TPU v7x, 256 devices: a whole 4x4x8 slice. The times are simulated.
256 devices in a mesh: island: 8 (over z_hi, x), fsdp: 32 (over y, z_lo, core).
Axes of the slice: x: 4, y: 4, z: 8 (z_hi: 2, z_lo: 4; z = z_hi * 4 + z_lo), core: 2. Of those that a mesh axis runs over, the one named last changes fastest.
Arguments:
- current: bfloat16 [8, 4, 8192, 512], P('island', None, 'fsdp'), may hold values from -6 to 6
- anchor: bfloat16 [4, 8192, 512], P(None, 'fsdp'), may hold values from -6 to 6
- momentum: float32 [4, 8192, 512], P(None, 'fsdp'), may hold values from -4 to 4
- tokens: bfloat16 [131072, 8192], P(('island', 'fsdp')), may hold values from -6 to 6
- fragment: int32 [1], replicated, may hold values from 0 to 3
Outputs:
- new_current: bfloat16 [8, 4, 8192, 512], P('island', None, 'fsdp')
- new_momentum: float32 [4, 8192, 512], P(None, 'fsdp')
- keys: bfloat16 [131072, 512], P(('island', 'fsdp'))
All inputs are finite; a program needn't handle non-finite values.
Results may differ from a plain program's by a relative error of at most 0.0049.
Values may be sent and summed in bfloat16 or wider, within the bound.
A program may use at most 64 MiB of HBM per device.

v0:
```python
import math

import jax
import jax.numpy as jnp
from jax import lax
from jax.sharding import PartitionSpec as P

D = 8192


outer_momentum = 0.9
outer_rate = 0.7
blend_local = 0.5


def synchronize(cur_layer, anc_layer, mom_layer, tokens):
    cur_full = cur_layer.astype(jnp.float32)
    anc_full = anc_layer.astype(jnp.float32)
    drift_local = cur_full - anc_full
    islands = lax.axis_size("island")
    drift_mean = lax.psum(drift_local, "island") / islands
    mom_next = outer_momentum * mom_layer + drift_mean
    global_new = anc_full + outer_rate * (outer_momentum * mom_next + drift_mean)
    blended = (blend_local * cur_full + (1.0 - blend_local) * global_new).astype(jnp.bfloat16)
    products = jnp.dot(
        tokens,
        lax.all_gather(blended, "fsdp", axis=0, tiled=True),
        preferred_element_type=jnp.float32,
    )
    return (blended, mom_next, products)


def local(current, anchor, momentum, tokens, fragment):
    slot_index = fragment[0]
    own_layers = current[0]
    cur_layer = lax.dynamic_index_in_dim(own_layers, slot_index, 0, keepdims=False)
    anc_layer = lax.dynamic_index_in_dim(anchor, slot_index, 0, keepdims=False)
    mom_layer = lax.dynamic_index_in_dim(momentum, slot_index, 0, keepdims=False)
    blended, mom_next, products = synchronize(cur_layer, anc_layer, mom_layer, tokens)
    new_layers = lax.dynamic_update_index_in_dim(own_layers, blended, slot_index, 0)
    new_momentum = lax.dynamic_update_index_in_dim(momentum, mom_next, slot_index, 0)
    keys = (products * (1.0 / math.sqrt(D))).astype(jnp.bfloat16)
    return (new_layers[None], new_momentum, keys)


def solution(mesh):
    placed = (
        P("island", None, "fsdp", None),
        P(None, "fsdp", None),
        P(None, "fsdp", None),
        P(("island", "fsdp"), None),
        P(),
    )
    return jax.shard_map(
        local,
        mesh=mesh,
        in_specs=placed,
        out_specs=(
            P("island", None, "fsdp", None),
            P(None, "fsdp", None),
            P(("island", "fsdp"), None),
        ),
        check_vma=False,
    )
```

profile of v0, /device:TPU:1, one launch (start us, length us, event | category | flops | bytes accessed | tf_op | source)
XLA Modules:
  0.0 212.6 jit_solution(6661155105144402321)
XLA Ops:
  7.2 0.0 all-reduce.2.cloned.1.call-start
  7.2 1.2 copy.15
  8.4 1.6 copy.16
  10.7 1.8 convert_subtract_fusion
  12.5 0.0 all-reduce.2.cloned.1.call-update
  12.5 0.0 all-gather.2.cloned.1.call-start
  12.6 107.3 %all-reduce.2.cloned.1.call-done = f32[256,512]{1,0:T(8,128)} async-done(((f32[256,512]{1,0:T(8,128)}), f32[256,512]{1,0:T(8,128)}) %all-reduce.2.cloned.1.call-update) | async-done | bytes 524304 | tf_op jit(solution)/shard_map/psum | solution.py:21
  119.9 2.2 %bitcast_add_fusion = (f32[256,512]{1,0:T(8,128)}, bf16[256,512]{1,0:T(8,128)(2,1)}) fusion(f32[4,256,512]{2,1,0:T(8,128)S(1)} %copy.16, s32[]{:T(128)S(6)} %select_n.11, f32[256,512]{1,0:T(8,128)} %all-reduce.2.cloned.1.call-done, bf16[4,256,512]{2,1,0:T(8,128)(2,1)} %param.6, bf16[1,4,256,512]{3,2,1,0:T(8,128)(2,1)S(1)} %copy.15), kind=kLoop, calls=%fused_computation.9 | loop fusion | flops 1572864 | bytes 2359300 | tf_op jit(solution)/shard_map/add | solution.py:22
  122.1 0.0 all-gather.2.cloned.1.call-update
  122.1 1.0 bitcast_dynamic-update-slice_fusion.1
  123.1 0.0 copy-start.1
  123.1 1.5 bitcast_dynamic-update-slice_fusion
  124.6 0.0 copy-start
  124.6 68.0 %all-gather.2.cloned.1.call-done = bf16[8192,512]{1,0:T(8,128)(2,1)} async-done(((bf16[256,512]{1,0:T(8,128)(2,1)}), bf16[8192,512]{1,0:T(8,128)(2,1)}) %all-gather.2.cloned.1.call-update) | async-done | bytes 8388624 | tf_op jit(solution)/shard_map/all_gather | solution.py:27
  192.6 11.1 %fusion.1 = bf16[512,512]{0,1:T(8,128)(2,1)} fusion(bf16[8192,512]{1,0:T(8,128)(2,1)} %all-gather.2.cloned.1.call-done, bf16[512,8192]{1,0:T(8,128)(2,1)} %param.8), kind=kOutput, calls=%fused_computation.2 | convolution fusion | flops 4295491584 | bytes 17301504 | tf_op jit(solution)/shard_map/dot_general | solution.py:25
  203.7 0.0 copy-done.1
  203.7 0.0 copy-done
  203.7 2.0 copy.8
Async XLA Ops:
  7.2 112.7 %all-reduce.2.cloned.1.call-start = ((), (), s32[]{:S(2)}) async-start(), calls=%async_computation | async-start | bytes 1048576 | tf_op jit(solution)/shard_map/psum | solution.py:21
  12.5 180.0 %all-gather.2.cloned.1.call-start = ((), (), s32[]{:S(2)}) async-start(), calls=%async_computation.1 | async-start | bytes 8650752 | tf_op jit(solution)/shard_map/all_gather | solution.py:27
  123.1 80.6 %copy-start.1 = (bf16[1,4,256,512]{3,2,1,0:T(8,128)(2,1)}, bf16[1,4,256,512]{3,2,1,0:T(8,128)(2,1)S(1)}, u32[]{:S(2)}) copy-start(bf16[1,4,256,512]{3,2,1,0:T(8,128)(2,1)S(1)} %bitcast_dynamic-update-slice_fusion.1) | copy-start | bytes 3145732
  124.6 79.2 %copy-start = (f32[4,256,512]{2,1,0:T(8,128)}, f32[4,256,512]{2,1,0:T(8,128)S(1)}, u32[]{:S(2)}) copy-start(f32[4,256,512]{2,1,0:T(8,128)S(1)} %bitcast_dynamic-update-slice_fusion) | copy-start | bytes 6291460
Sparse Core Ops, SparseCore 0:
  12.7 107.1 all-reduce.1
  122.2 70.2 all-gather.1
where the time goes:
time: 213 us
  waiting for transfers between devices  175 us (82%)
  between operations  14.7 us (7%)
  matrix products  11.1 us (5%)
  local copies, waits for them, and re-layouts  7.31 us (3%)
  other arithmetic  4.03 us (2%)
    psum x1, waiting for transfers between devices, synchronize(): drift_mean = lax.psum(drift_local, 'island') / islands  107 us
    all_gather x1, waiting for transfers between devices, synchronize(): lax.all_gather(blended, 'fsdp', axis=0, tiled=True)  68 us
    dot_general x1, matrix products, synchronize(): jnp.dot(tokens, lax.all_gather(blended, 'fsdp', axis=0, tiled=True), pref...  11.1 us
    unnamed x7, local copies, waits for them, and re-layouts  4.88 us
  transfers between devices with their start and end apart: 2, of which 2 were waited for; matrix products, arithmetic and copies ran while one was open for 1% of the time, Pallas kernels for 0%

commit v1 on v0

v1 whole, which is shorter than its diff:
```python
import math

import jax
import jax.numpy as jnp
from jax import lax
from jax.experimental import pallas as pl
from jax.experimental.pallas import tpu as pltpu
from jax.sharding import PartitionSpec as P

D = 8192
WIDTH = 512
ROWS = 256
G = 16
CHUNKS = 4
MESH = pl.DeviceIdType.MESH

outer_momentum = 0.9
outer_rate = 0.7
blend_local = 0.5

PIECES = ((0, 4), (4, 4), (8, 5), (13, 3))
PARTS = (((0, 2), (2, 2)), ((4, 2), (6, 2)), ((8, 3), (11, 2)), ((13, 1), (14, 2)))
YP = 3
ZROWS = 13 * G
YROWS = 3 * G
PLUS = [sum(PARTS[p][0][1] for p in range(3)) * G, PARTS[YP][0][1] * G]
MINUS = [sum(PARTS[p][1][1] for p in range(3)) * G, PARTS[YP][1][1] * G]


def kernel(frag, cur_hbm, anc_hbm, mom_hbm, tok_hbm,
           keys, blend_hbm, momn_hbm,
           cur4, anc4, mom4, tok, w, cur, raw, s_out, s_in, drift, momn, acc,
           load_sem, out_sem, raw_ss, raw_rs, s_ss, s_rs, d_ss, d_rs,
           g_ss, g_rs, sib_ss, sib_rs):
    island = lax.axis_index("island")
    fsdp = lax.axis_index("fsdp")
    zh, x = island // 4, island % 4
    y, z, c = fsdp // 8, (fsdp // 2) % 4, fsdp % 2

    def at(zh_, x_, y_, z_, c_):
        return (zh_ * 4 + x_, y_ * 8 + z_ * 2 + c_)

    y_up, y_dn, y_far = (y + 1) % 4, (y + 3) % 4, (y + 2) % 4
    has_up, has_dn = z < 3, z > 0
    z_up, z_dn = jnp.minimum(z + 1, 3), jnp.maximum(z - 1, 0)
    dev_yu, dev_yd = at(zh, x, y_up, z, c), at(zh, x, y_dn, z, c)
    dev_zu, dev_zd = at(zh, x, y, z_up, c), at(zh, x, y, z_dn, c)
    dev_sib = at(zh, x, y, z, 1 - c)
    dev_far = at(1 - zh, x, y, z, c)
    dev_x = [at(zh, (x + d) % 4, y, z, c) for d in (1, 2, 3)]

    loads = [
        pltpu.make_async_copy(cur_hbm.at[0], cur4, load_sem.at[0]),
        pltpu.make_async_copy(anc_hbm, anc4, load_sem.at[1]),
        pltpu.make_async_copy(mom_hbm, mom4, load_sem.at[2]),
        pltpu.make_async_copy(tok_hbm, tok, load_sem.at[3]),
    ]
    for load in loads:
        load.start()

    barrier = pltpu.get_barrier_semaphore()
    for dev in (*dev_x, dev_far, dev_yu, dev_yd, dev_sib):
        pl.semaphore_signal(barrier, inc=1, device_id=dev, device_id_type=MESH)

    @pl.when(has_up)
    def _():
        pl.semaphore_signal(barrier, inc=1, device_id=dev_zu, device_id_type=MESH)

    @pl.when(has_dn)
    def _():
        pl.semaphore_signal(barrier, inc=1, device_id=dev_zd, device_id_type=MESH)

    ends = jnp.where(has_up, 1, 0) + jnp.where(has_dn, 1, 0)

    fr = frag[0]
    loads[0].wait()
    cur[...] = cur4[fr].reshape(16, G, WIDTH)
    pl.semaphore_wait(barrier, 7 + ends)

    def remote(src, dst, ss, rs, dev):
        return pltpu.make_async_remote_copy(
            src_ref=src, dst_ref=dst, send_sem=ss, recv_sem=rs,
            device_id=dev, device_id_type=MESH,
        )

    def raw_copy(k, d):
        to = (x + d + 1) % 4
        return remote(cur.at[4 * k + to], raw.at[d, k], raw_ss.at[d, k], raw_rs.at[d, k], dev_x[d])

    def s_copy(k):
        return remote(s_out.at[k], s_in.at[k], s_ss.at[k], s_rs.at[k], dev_far)

    def d_copy(k, d):
        mine = 4 * k + x
        return remote(drift.at[mine], drift.at[mine], d_ss.at[d, k], d_rs.at[d, k], dev_x[d])

    def d_wait(k, d):
        theirs = 4 * k + (x + 3 - d) % 4
        remote(drift.at[theirs], drift.at[theirs], d_ss.at[d, k], d_rs.at[d, k], dev_x[d]).wait_recv()

    for k in range(CHUNKS):
        for d in range(3):
            raw_copy(k, d).start()
    acc[...] = jnp.zeros_like(acc)
    loads[1].wait()
    for k in range(CHUNKS):
        for d in range(3):
            raw_copy(k, d).wait_recv()
        mine = 4 * k + x
        anc = anc4[fr, pl.ds(pl.multiple_of(mine * G, G), G), :].astype(jnp.float32)
        total = cur[mine].astype(jnp.float32) - anc
        for d in range(3):
            total += raw[d, k].astype(jnp.float32) - anc
        s_out[k] = total.astype(jnp.bfloat16)
        s_copy(k).start()

    def exchange(k):
        s_copy(k).wait_recv()
        both = s_out[k].astype(jnp.float32) + s_in[k].astype(jnp.float32)
        drift[4 * k + x] = (both * 0.125).astype(jnp.bfloat16)
        for d in range(3):
            d_copy(k, d).start()

    def block(oy, oz, first, count):
        return w.at[oy * 8 + oz * 2 + c, pl.ds(first, count)]

    def go(t, dev, oy, oz, p, h, span):
        ref = block(oy, oz, *span)
        return remote(ref, ref, g_ss.at[t], g_rs.at[oy * 4 + oz, p, h], dev)

    def arrive(oy, oz, p, h, span):
        go(0, dev_yu, oy, oz, p, h, span).wait_recv()

    def to_y(oy, oz, p):
        go(0, dev_yu, oy, oz, p, 0, PIECES[p]).start()
        go(1, dev_yd, oy, oz, p, 0, PIECES[p]).start()

    def to_z(oy, oz, p, up, dn):
        if up is not None:
            @pl.when(up)
            def _():
                go(2, dev_zu, oy, oz, p, 0, PIECES[p]).start()
        if dn is not None:
            @pl.when(dn)
            def _():
                go(3, dev_zd, oy, oz, p, 0, PIECES[p]).start()

    def sib(oy, oz, half):
        ref = block(oy, oz, 8 * half, 8)
        return remote(ref, ref, sib_ss.at[0], sib_rs.at[oy * 4 + oz, half], dev_sib)

    def sib_wait(oy, oz, half):
        ref = w.at[oy * 8 + oz * 2 + 1 - c, pl.ds(8 * half, 8)]
        remote(ref, ref, sib_ss.at[0], sib_rs.at[oy * 4 + oz, half], dev_sib).wait_recv()

    outs = [
        pltpu.make_async_copy(w.at[fsdp], blend_hbm, out_sem.at[0]),
        pltpu.make_async_copy(momn, momn_hbm, out_sem.at[1]),
    ]

    def own(k):
        for d in range(3):
            d_wait(k, d)
        rows = pl.ds(64 * k, 64)
        anc = anc4[fr, rows, :].astype(jnp.float32)
        mean = drift[4 * k:4 * k + 4].reshape(64, WIDTH).astype(jnp.float32)
        nxt = outer_momentum * mom4[fr, rows, :] + mean
        momn[rows, :] = nxt
        glob = anc + outer_rate * (outer_momentum * nxt + mean)
        local = cur[4 * k:4 * k + 4].reshape(64, WIDTH).astype(jnp.float32)
        new = (blend_local * local + (1.0 - blend_local) * glob).astype(jnp.bfloat16)
        w[fsdp, 4 * k:4 * k + 4] = new.reshape(4, G, WIDTH)

    def send_own(p):
        to_z(y, z, p, has_up, has_dn)
        to_y(y, z, p)

    exchange(0)
    exchange(1)
    loads[2].wait()
    own(0)
    send_own(0)
    exchange(2)
    own(1)
    send_own(1)
    sib(y, z, 0).start()
    exchange(3)
    own(2)
    own(3)
    send_own(2)
    to_y(y, z, YP)
    sib(y, z, 1).start()
    for out in outs:
        out.start()

    low = z < 2
    zm = jnp.where(low, z, 3 - z)

    def zo(j):
        if j == 0:
            return z
        m = j if j > 1 else jnp.where(zm == 0, 1, 0)
        return jnp.where(low, m, 3 - m)

    oz = [zo(j) for j in range(4)]
    go_up = [None] + [(oz[j] < z) & has_up for j in (1, 2, 3)]
    go_dn = [None] + [(oz[j] > z) & has_dn for j in (1, 2, 3)]

    def zz(j, p):
        arrive(y, oz[j], p, 0, PIECES[p])
        to_z(y, oz[j], p, go_up[j], go_dn[j])
        to_y(y, oz[j], p)

    def zy(j, p):
        arrive(y_dn, oz[j], p, 0, PIECES[p])
        go(0, dev_yu, y_dn, oz[j], p, 0, PARTS[p][0]).start()
        arrive(y_up, oz[j], p, 0, PIECES[p])
        go(1, dev_yd, y_up, oz[j], p, 1, PARTS[p][1]).start()

    def zy_far(j, p):
        arrive(y_far, oz[j], p, 0, PARTS[p][0])
        arrive(y_far, oz[j], p, 1, PARTS[p][1])

    def yz(j):
        for oy in (y, y_up, y_dn, y_far):
            arrive(oy, oz[j], YP, 0, PIECES[YP])
            to_z(oy, oz[j], YP, go_up[j], go_dn[j])

    def sib_group(j, half):
        for oy in (y, y_up, y_dn, y_far):
            if j == 0 and oy is y:
                continue
            sib(oy, oz[j], half).start()

    def multiply(j, half):
        def unit(oy, _):
            sib_wait(oy, oz[j], half)
            f = oy * 8 + oz[j] * 2
            a0 = tok[:, pl.ds(pl.multiple_of(f * ROWS + half * 128, 128), 128)]
            a1 = tok[:, pl.ds(pl.multiple_of((f + 1) * ROWS + half * 128, 128), 128)]
            b0 = w[f, 8 * half:8 * half + 8].reshape(128, WIDTH)
            b1 = w[f + 1, 8 * half:8 * half + 8].reshape(128, WIDTH)
            acc[...] += jnp.dot(
                jnp.concatenate([a0, a1], axis=1), jnp.concatenate([b0, b1], axis=0),
                preferred_element_type=jnp.float32,
            )
            return 0

        lax.fori_loop(0, 4, unit, 0)

    for p in range(3):
        zz(1, p)
        zy(0, p)
    zy(0, YP)
    for p in range(3):
        zz(2, p)
    for p in range(3):
        zz(3, p)
        zy(1, p)
    to_z(y, z, YP, has_up, has_dn)
    to_z(y_up, z, YP, has_up, has_dn)
    to_z(y_dn, z, YP, has_up, has_dn)
    for p in range(4):
        zy_far(0, p)
    to_z(y_far, z, YP, has_up, has_dn)
    sib_group(0, 0)
    sib_group(0, 1)
    loads[3].wait()
    multiply(0, 0)
    yz(1)
    multiply(0, 1)
    for p in range(3):
        zy(2, p)
    zy_far(1, 0)
    zy_far(1, 1)
    zy_far(1, 2)
    sib_group(1, 0)
    sib_group(1, 1)
    multiply(1, 0)
    yz(2)
    multiply(1, 1)
    for p in range(3):
        zy(3, p)
    for p in range(3):
        zy_far(2, p)
    sib_group(2, 0)
    sib_group(2, 1)
    multiply(2, 0)
    multiply(2, 1)
    zy_far(3, 0)
    zy_far(3, 1)
    sib_group(3, 0)
    multiply(3, 0)
    yz(3)
    zy_far(3, 2)
    sib_group(3, 1)
    multiply(3, 1)
    keys[...] = (acc[...] * (1.0 / math.sqrt(D))).astype(jnp.bfloat16)

    for k in range(CHUNKS):
        s_copy(k).wait_send()
        for d in range(3):
            raw_copy(k, d).wait_send()
            d_copy(k, d).wait_send()

    flat = w.reshape(32 * 16 * G, WIDTH)

    def sent(sem, rows):
        ref = flat.at[pl.ds(0, rows)]
        remote(ref, ref, sem, g_rs.at[0, 0, 0], dev_sib).wait_send()

    sent(g_ss.at[0], 4 * (ZROWS + PLUS[0]) + YROWS + PLUS[1])
    sent(g_ss.at[1], 4 * (ZROWS + MINUS[0]) + YROWS + MINUS[1])
    for at_z in range(3):
        @pl.when(z == at_z)
        def _(at_z=at_z):
            sent(g_ss.at[2], (at_z + 1) * (ZROWS + 4 * YROWS))

        @pl.when(z == 3 - at_z)
        def _(at_z=at_z):
            sent(g_ss.at[3], (at_z + 1) * (ZROWS + 4 * YROWS))
    sent(sib_ss.at[0], 16 * ROWS)
    for out in outs:
        out.wait()


def fused(current, anchor, momentum, tokens, fragment):
    bf, f32 = jnp.bfloat16, jnp.float32
    dma = pltpu.SemaphoreType.DMA
    return pl.pallas_call(
        kernel,
        out_shape=(
            jax.ShapeDtypeStruct((512, WIDTH), bf),
            jax.ShapeDtypeStruct((16, G, WIDTH), bf),
            jax.ShapeDtypeStruct((ROWS, WIDTH), f32),
        ),
        in_specs=[pl.BlockSpec(memory_space=pltpu.SMEM)] + [pl.BlockSpec(memory_space=pl.ANY)] * 4,
        out_specs=(
            pl.BlockSpec(memory_space=pltpu.VMEM),
            pl.BlockSpec(memory_space=pl.ANY),
            pl.BlockSpec(memory_space=pl.ANY),
        ),
        scratch_shapes=[
            pltpu.VMEM((4, ROWS, WIDTH), bf),
            pltpu.VMEM((4, ROWS, WIDTH), bf),
            pltpu.VMEM((4, ROWS, WIDTH), f32),
            pltpu.VMEM((512, D), bf),
            pltpu.VMEM((32, 16, G, WIDTH), bf),
            pltpu.VMEM((16, G, WIDTH), bf),
            pltpu.VMEM((3, CHUNKS, G, WIDTH), bf),
            pltpu.VMEM((CHUNKS, G, WIDTH), bf),
            pltpu.VMEM((CHUNKS, G, WIDTH), bf),
            pltpu.VMEM((16, G, WIDTH), bf),
            pltpu.VMEM((ROWS, WIDTH), f32),
            pltpu.VMEM((512, WIDTH), f32),
            dma((4,)), dma((2,)),
            dma((3, CHUNKS)), dma((3, CHUNKS)), dma((CHUNKS,)), dma((CHUNKS,)),
            dma((3, CHUNKS)), dma((3, CHUNKS)),
            dma((4,)), dma((16, 4, 2)), dma((1,)), dma((16, 2)),
        ],
        compiler_params=pltpu.CompilerParams(
            collective_id=0, has_side_effects=True, vmem_limit_bytes=48 * 2**20
        ),
    )(fragment, current, anchor, momentum, tokens)


def place_kernel(frag, cur, mom, keys_in, blended, momn, new_cur, new_mom, keys, sem):
    fr = frag[0]
    copy = pltpu.make_async_copy(keys_in, keys, sem.at[8])
    copy.start()
    for i in range(4):
        @pl.when(fr == i)
        def _(i=i):
            pltpu.make_async_copy(momn, new_mom.at[i], sem.at[i]).start()
            pltpu.make_async_copy(blended, new_cur.at[0, i], sem.at[4 + i]).start()

        @pl.when(fr != i)
        def _(i=i):
            pltpu.make_async_copy(mom.at[i], new_mom.at[i], sem.at[i]).start()
            pltpu.make_async_copy(cur.at[0, i], new_cur.at[0, i], sem.at[4 + i]).start()
    for i in range(4):
        pltpu.make_async_copy(mom.at[i], new_mom.at[i], sem.at[i]).wait()
        pltpu.make_async_copy(cur.at[0, i], new_cur.at[0, i], sem.at[4 + i]).wait()
    copy.wait()


def local(current, anchor, momentum, tokens, fragment):
    keys, blended, mom_next = fused(current, anchor, momentum, tokens, fragment)
    return pl.pallas_call(
        place_kernel,
        out_shape=(
            jax.ShapeDtypeStruct(current.shape, current.dtype),
            jax.ShapeDtypeStruct(momentum.shape, momentum.dtype),
            jax.ShapeDtypeStruct(keys.shape, keys.dtype),
        ),
        in_specs=[pl.BlockSpec(memory_space=pltpu.SMEM)] + [pl.BlockSpec(memory_space=pl.ANY)] * 5,
        out_specs=tuple([pl.BlockSpec(memory_space=pl.ANY)] * 3),
        scratch_shapes=[pltpu.SemaphoreType.DMA((9,))],
    )(fragment, current, momentum, keys, blended.reshape(ROWS, WIDTH), mom_next)


def solution(mesh):
    placed = (
        P("island", None, "fsdp", None),
        P(None, "fsdp", None),
        P(None, "fsdp", None),
        P(("island", "fsdp"), None),
        P(),
    )
    return jax.shard_map(
        local,
        mesh=mesh,
        in_specs=placed,
        out_specs=(
            P("island", None, "fsdp", None),
            P(None, "fsdp", None),
            P(("island", "fsdp"), None),
        ),
        check_vma=False,
    )
```

time: 213 us -> 190 us (0.89)
  Pallas kernels: 0 us -> 182 us
  waiting for transfers between devices: 175 us -> 0 us
  between operations: 14.7 us -> 1.31 us
  matrix products: 11.1 us -> 0 us
  other arithmetic: 4.03 us -> 0 us
    pallas_call x0 -> x2, Pallas kernels: none -> 182 us  [the longest x1 112 us: local(): pl.pallas_call(place_kernel, out_shape=(jax.ShapeDtypeStruct(current.shap...]
    psum x1 -> x0, waiting for transfers between devices: 107 us -> none  [synchronize(): drift_mean = lax.psum(drift_local, 'island') / islands]
    all_gather x1 -> x0, waiting for transfers between devices: 68 us -> none  [synchronize(): lax.all_gather(blended, 'fsdp', axis=0, tiled=True)]
    dot_general x1 -> x0, matrix products: 11.1 us -> none  [synchronize(): jnp.dot(tokens, lax.all_gather(blended, 'fsdp', axis=0, tiled=True), pref...]
    dynamic_update_slice x2 -> x0, local copies, waits for them, and re-layouts: 2.44 us -> none  [the longest x1 1.46 us: local(): lax.dynamic_update_index_in_dim(momentum, mom_next, slot_index, 0)]
    add x1 -> x0, other arithmetic: 2.2 us -> none  [synchronize(): mom_next = outer_momentum * mom_layer + drift_mean]
    unnamed x7 -> x12, local copies, waits for them, and re-layouts: 4.88 us -> 6.32 us
  transfers between devices with their start and end apart: 2 -> 0, of which waited for: 2 -> 0; matrix products, arithmetic and copies ran while one was open for 1% -> 0% of each run, Pallas kernels for 0% -> 0%
where the time goes in v1:
time: 190 us; the launch traced here: 189 us
  Pallas kernels  182 us (96%)
  local copies, waits for them, and re-layouts  6.32 us (3%)
    pallas_call x1, Pallas kernels, local(): pl.pallas_call(place_kernel, out_shape=(jax.ShapeDtypeStruct(current.shap...  112 us
    pallas_call x1, Pallas kernels, fused(): pl.pallas_call(kernel, out_shape=(jax.ShapeDtypeStruct((512, WIDTH), bf),...  69.3 us
    unnamed x12, local copies, waits for them, and re-layouts  6.32 us

profile of v1, /device:TPU:1, one launch (start us, length us, event | category | flops | bytes accessed | tf_op | source)
XLA Modules:
  0.0 189.3 jit_solution(1266893844820537977)
XLA Ops:
  1.3 0.0 copy-start
  1.3 1.6 copy-done
  2.9 0.0 copy-start.1
  2.9 1.2 copy-done.1
  4.1 0.0 copy-start.2
  4.1 1.2 copy-done.2
  5.3 69.3 %shard_map.76 = (bf16[512,512]{1,0:T(8,128)(2,1)S(1)}, bf16[16,16,512]{2,1,0:T(8,128)(2,1)S(1)}, f32[256,512]{1,0:T(8,128)S(1)}) custom-call(s32[1]{0:T(128)S(6)} %copy.8.frag, bf16[1,4,256,512]{3,2,1,0:T(8,128)(2,1)S(1)} %copy-done.1, bf16[4,256,512]{2,1,0:T(8,128)(2,1)S(1)} %copy-done.2, f32[4,256,512]{2,1,0:T(8,128)S(1)} %copy-done, bf16[512,8192]{1,0:T(8,128)(2,1)} %tok_hbm.1), custom_call_target="tpu_custom_call" | custom-call | tf_op jit(solution)/shard_map/pallas_call | solution.py:330
  74.7 0.0 copy-start.3
  74.7 0.8 copy-done.3
  75.5 0.0 copy-start.4
  75.5 0.8 copy-done.4
  76.3 0.0 copy-start.5
  76.3 0.7 copy-done.5
  77.0 112.4 %shard_map.77 = (bf16[1,4,256,512]{3,2,1,0:T(8,128)(2,1)}, f32[4,256,512]{2,1,0:T(8,128)}, bf16[512,512]{1,0:T(8,128)(2,1)}) custom-call(s32[1]{0:T(128)S(6)} %copy.8.frag, bf16[1,4,256,512]{3,2,1,0:T(8,128)(2,1)} %cur.1, f32[4,256,512]{2,1,0:T(8,128)} %mom.1, bf16[512,512]{1,0:T(8,128)(2,1)} %copy-done.3, bf16[256,512]{1,0:T(8,128)(2,1)} %bitcast.1, ...), custom_call_target="tpu_custom_call" | custom-call | tf_op jit(solution)/shard_map/pallas_call | solution.py:389
Async XLA Ops:
  1.3 1.6 copy-start
  2.9 1.2 copy-start.1
  4.1 1.2 copy-start.2
  74.7 0.8 copy-start.3
  75.5 0.8 copy-start.4
  76.3 0.7 copy-start.5

commit v2 on v1

--- a/solution.py
+++ b/solution.py
@@ -13,6 +13,7 @@
 G = 16
 CHUNKS = 4
 MESH = pl.DeviceIdType.MESH
+VMEM = 60 * 2**20
 
 outer_momentum = 0.9
 outer_rate = 0.7
@@ -28,8 +29,8 @@
 
 
 def kernel(frag, cur_hbm, anc_hbm, mom_hbm, tok_hbm,
-           keys, blend_hbm, momn_hbm,
-           cur4, anc4, mom4, tok, w, cur, raw, s_out, s_in, drift, momn, acc,
+           keys, cur_out, mom_out,
+           cur4, anc4, mom4, tok, w, cur, raw, s_out, s_in, drift, keys_v, acc,
            load_sem, out_sem, raw_ss, raw_rs, s_ss, s_rs, d_ss, d_rs,
            g_ss, g_rs, sib_ss, sib_rs):
     island = lax.axis_index("island")
@@ -117,7 +118,7 @@
     def exchange(k):
         s_copy(k).wait_recv()
         both = s_out[k].astype(jnp.float32) + s_in[k].astype(jnp.float32)
-        drift[4 * k + x] = (both * 0.125).astype(jnp.bfloat16)
+        drift[4 * k + x] = both * 0.125
         for d in range(3):
             d_copy(k, d).start()
 
@@ -154,8 +155,8 @@
         remote(ref, ref, sib_ss.at[0], sib_rs.at[oy * 4 + oz, half], dev_sib).wait_recv()
 
     outs = [
-        pltpu.make_async_copy(w.at[fsdp], blend_hbm, out_sem.at[0]),
-        pltpu.make_async_copy(momn, momn_hbm, out_sem.at[1]),
+        pltpu.make_async_copy(cur4, cur_out.at[0], out_sem.at[0]),
+        pltpu.make_async_copy(mom4, mom_out, out_sem.at[1]),
     ]
 
     def own(k):
@@ -163,13 +164,20 @@
             d_wait(k, d)
         rows = pl.ds(64 * k, 64)
         anc = anc4[fr, rows, :].astype(jnp.float32)
-        mean = drift[4 * k:4 * k + 4].reshape(64, WIDTH).astype(jnp.float32)
+        mean = drift[4 * k:4 * k + 4].reshape(64, WIDTH)
         nxt = outer_momentum * mom4[fr, rows, :] + mean
-        momn[rows, :] = nxt
         glob = anc + outer_rate * (outer_momentum * nxt + mean)
         local = cur[4 * k:4 * k + 4].reshape(64, WIDTH).astype(jnp.float32)
         new = (blend_local * local + (1.0 - blend_local) * glob).astype(jnp.bfloat16)
         w[fsdp, 4 * k:4 * k + 4] = new.reshape(4, G, WIDTH)
+        return nxt
+
+    def place(k, nxt):
+        rows = pl.ds(64 * k, 64)
+        new = w[fsdp, 4 * k:4 * k + 4].reshape(64, WIDTH)
+        for i in range(4):
+            mom4[i, rows, :] = jnp.where(fr == i, nxt, mom4[i, rows, :])
+            cur4[i, rows, :] = jnp.where(fr == i, new, cur4[i, rows, :])
 
     def send_own(p):
         to_z(y, z, p, has_up, has_dn)
@@ -178,18 +186,20 @@
     exchange(0)
     exchange(1)
     loads[2].wait()
-    own(0)
+    nxt0 = own(0)
     send_own(0)
     exchange(2)
-    own(1)
+    nxt1 = own(1)
     send_own(1)
     sib(y, z, 0).start()
     exchange(3)
-    own(2)
-    own(3)
+    nxt2 = own(2)
+    nxt3 = own(3)
     send_own(2)
     to_y(y, z, YP)
     sib(y, z, 1).start()
+    for k, nxt in enumerate((nxt0, nxt1, nxt2, nxt3)):
+        place(k, nxt)
     for out in outs:
         out.start()
 
@@ -295,7 +305,9 @@
     zy_far(3, 2)
     sib_group(3, 1)
     multiply(3, 1)
-    keys[...] = (acc[...] * (1.0 / math.sqrt(D))).astype(jnp.bfloat16)
+    keys_v[...] = (acc[...] * (1.0 / math.sqrt(D))).astype(jnp.bfloat16)
+    last = pltpu.make_async_copy(keys_v, keys, out_sem.at[2])
+    last.start()
 
     for k in range(CHUNKS):
         s_copy(k).wait_send()
@@ -322,6 +334,7 @@
     sent(sib_ss.at[0], 16 * ROWS)
     for out in outs:
         out.wait()
+    last.wait()
 
 
 def fused(current, anchor, momentum, tokens, fragment):
@@ -331,15 +344,11 @@
         kernel,
         out_shape=(
             jax.ShapeDtypeStruct((512, WIDTH), bf),
-            jax.ShapeDtypeStruct((16, G, WIDTH), bf),
-            jax.ShapeDtypeStruct((ROWS, WIDTH), f32),
+            jax.ShapeDtypeStruct((1, 4, ROWS, WIDTH), bf),
+            jax.ShapeDtypeStruct((4, ROWS, WIDTH), f32),
         ),
-        in_specs=[pl.BlockSpec(memory_space=pltpu.SMEM)] + [pl.BlockSpec(memory_space=pl.ANY)] * 4,
-        out_specs=(
-            pl.BlockSpec(memory_space=pltpu.VMEM),
-            pl.BlockSpec(memory_space=pl.ANY),
-            pl.BlockSpec(memory_space=pl.ANY),
-        ),
+        in_specs=[pl.BlockSpec(memory_space=pltpu.SMEM)] + [pl.BlockSpec(memory_space=pltpu.HBM)] * 4,
+        out_specs=tuple([pl.BlockSpec(memory_space=pl.ANY)] * 3),
         scratch_shapes=[
             pltpu.VMEM((4, ROWS, WIDTH), bf),
             pltpu.VMEM((4, ROWS, WIDTH), bf),
@@ -350,53 +359,42 @@
             pltpu.VMEM((3, CHUNKS, G, WIDTH), bf),
             pltpu.VMEM((CHUNKS, G, WIDTH), bf),
             pltpu.VMEM((CHUNKS, G, WIDTH), bf),
-            pltpu.VMEM((16, G, WIDTH), bf),
-            pltpu.VMEM((ROWS, WIDTH), f32),
+            pltpu.VMEM((16, G, WIDTH), f32),
+            pltpu.VMEM((512, WIDTH), bf),
             pltpu.VMEM((512, WIDTH), f32),
-            dma((4,)), dma((2,)),
+            dma((4,)), dma((3,)),
             dma((3, CHUNKS)), dma((3, CHUNKS)), dma((CHUNKS,)), dma((CHUNKS,)),
             dma((3, CHUNKS)), dma((3, CHUNKS)),
             dma((4,)), dma((16, 4, 2)), dma((1,)), dma((16, 2)),
         ],
         compiler_params=pltpu.CompilerParams(
-            collective_id=0, has_side_effects=True, vmem_limit_bytes=48 * 2**20
+            collective_id=0, has_side_effects=True, vmem_limit_bytes=VMEM
         ),
     )(fragment, current, anchor, momentum, tokens)
 
 
-def place_kernel(frag, cur, mom, keys_in, blended, momn, new_cur, new_mom, keys, sem):
-    fr = frag[0]
-    copy = pltpu.make_async_copy(keys_in, keys, sem.at[8])
-    copy.start()
-    for i in range(4):
-        @pl.when(fr == i)
-        def _(i=i):
-            pltpu.make_async_copy(momn, new_mom.at[i], sem.at[i]).start()
-            pltpu.make_async_copy(blended, new_cur.at[0, i], sem.at[4 + i]).start()
-
-        @pl.when(fr != i)
-        def _(i=i):
-            pltpu.make_async_copy(mom.at[i], new_mom.at[i], sem.at[i]).start()
-            pltpu.make_async_copy(cur.at[0, i], new_cur.at[0, i], sem.at[4 + i]).start()
-    for i in range(4):
-        pltpu.make_async_copy(mom.at[i], new_mom.at[i], sem.at[i]).wait()
-        pltpu.make_async_copy(cur.at[0, i], new_cur.at[0, i], sem.at[4 + i]).wait()
-    copy.wait()
+def place_kernel(cur_in, mom_in, keys_in, cur, mom, keys):
+    cur[...] = cur_in[...]
+    mom[...] = mom_in[...]
+    keys[...] = keys_in[...]
 
 
 def local(current, anchor, momentum, tokens, fragment):
-    keys, blended, mom_next = fused(current, anchor, momentum, tokens, fragment)
+    keys, new_current, new_momentum = fused(current, anchor, momentum, tokens, fragment)
+    shapes = [jax.ShapeDtypeStruct(a.shape, a.dtype) for a in (new_current, new_momentum, keys)]
+    specs = [
+        pl.BlockSpec((1, 4, ROWS // 2, WIDTH), lambda i: (0, 0, i, 0)),
+        pl.BlockSpec((4, ROWS // 2, WIDTH), lambda i: (0, i, 0)),
+        pl.BlockSpec((ROWS, WIDTH), lambda i: (i, 0)),
+    ]
     return pl.pallas_call(
         place_kernel,
-        out_shape=(
-            jax.ShapeDtypeStruct(current.shape, current.dtype),
-            jax.ShapeDtypeStruct(momentum.shape, momentum.dtype),
-            jax.ShapeDtypeStruct(keys.shape, keys.dtype),
-        ),
-        in_specs=[pl.BlockSpec(memory_space=pltpu.SMEM)] + [pl.BlockSpec(memory_space=pl.ANY)] * 5,
-        out_specs=tuple([pl.BlockSpec(memory_space=pl.ANY)] * 3),
-        scratch_shapes=[pltpu.SemaphoreType.DMA((9,))],
-    )(fragment, current, momentum, keys, blended.reshape(ROWS, WIDTH), mom_next)
+        out_shape=tuple(shapes),
+        grid=(2,),
+        in_specs=specs,
+        out_specs=tuple(specs),
+        compiler_params=pltpu.CompilerParams(vmem_limit_bytes=VMEM),
+    )(new_current, new_momentum, keys)
 
 
 def solution(mesh):

time: 190 us -> 75.9 us (0.40)
  Pallas kernels: 182 us -> 74.5 us
  local copies, waits for them, and re-layouts: 6.32 us -> 0 us
    pallas_call x1, Pallas kernels: 112 us -> 3.39 us  [local(): pl.pallas_call(place_kernel, out_shape=tuple(shapes), grid=(2,), in_specs...]
    unnamed x12 -> x0, local copies, waits for them, and re-layouts: 6.32 us -> none
where the time goes in v2:
time: 75.9 us; the launch traced here: 75.8 us
  Pallas kernels  74.5 us (98%)
  between operations  1.29 us (2%)
    pallas_call x1, Pallas kernels, fused(): pl.pallas_call(kernel, out_shape=(jax.ShapeDtypeStruct((512, WIDTH), bf),...  71.2 us
    pallas_call x1, Pallas kernels, local(): pl.pallas_call(place_kernel, out_shape=tuple(shapes), grid=(2,), in_specs...  3.39 us

profile of v2, /device:TPU:1, one launch (start us, length us, event | category | flops | bytes accessed | tf_op | source)
XLA Modules:
  0.0 75.8 jit_solution(2461502678498746617)
XLA Ops:
  1.3 71.2 %shard_map.76 = (bf16[512,512]{1,0:T(8,128)(2,1)}, bf16[1,4,256,512]{3,2,1,0:T(8,128)(2,1)}, f32[4,256,512]{2,1,0:T(8,128)}) custom-call(s32[1]{0:T(128)S(6)} %copy.8.frag, bf16[1,4,256,512]{3,2,1,0:T(8,128)(2,1)} %cur_hbm.1, bf16[4,256,512]{2,1,0:T(8,128)(2,1)} %anc_hbm.1, f32[4,256,512]{2,1,0:T(8,128)} %mom_hbm.1, bf16[512,8192]{1,0:T(8,128)(2,1)} %tok_hbm.1), custom_call_target="tpu_custom_call" | custom-call | tf_op jit(solution)/shard_map/pallas_call | solution.py:343
  72.4 3.4 %shard_map.77 = (bf16[1,4,256,512]{3,2,1,0:T(8,128)(2,1)}, f32[4,256,512]{2,1,0:T(8,128)}, bf16[512,512]{1,0:T(8,128)(2,1)}) custom-call(bf16[1,4,256,512]{3,2,1,0:T(8,128)(2,1)} %get-tuple-element.6.cur_in, f32[4,256,512]{2,1,0:T(8,128)} %get-tuple-element.7.mom_in, bf16[512,512]{1,0:T(8,128)(2,1)} %get-tuple-element.8.keys_in), custom_call_target="tpu_custom_call" | custom-call | tf_op jit(solution)/shard_map/pallas_call | solution.py:390

commit v3 on v0

v3 whole, which is shorter than its diff:
```python
import math

import jax
import jax.numpy as jnp
from jax import lax
from jax.experimental import pallas as pl
from jax.experimental.pallas import tpu as pltpu
from jax.sharding import PartitionSpec as P

D = 8192
WIDTH = 512
ROWS = 256
G = 16
CHUNKS = 4
MESH = pl.DeviceIdType.MESH
VMEM = 60 * 2**20

outer_momentum = 0.9
outer_rate = 0.7
blend_local = 0.5

HALF = 8
A_PIECES, A_PARTS = ((0, 5), (5, 3)), (((0, 3), (3, 2)), ((5, 1), (6, 2)))
B_PIECES, B_PARTS = ((0, 4), (4, 4)), (((0, 2), (2, 2)), ((4, 2), (6, 2)))
ZP, YP = 0, 1


def kernel(frag, cur_hbm, anc_hbm, mom_hbm, tok_hbm,
           keys, cur_out, mom_out,
           cur4, anc4, mom4, tok, ra, wa, wb, gb, cur, raw, s_out, s_in, drift, keys_v, acc,
           load_sem, out_sem, raw_ss, raw_rs, s_ss, s_rs, d_ss, d_rs,
           send_sem, a_rs, b_rs, g_rs, x_rs, sib_rs):
    island = lax.axis_index("island")
    fsdp = lax.axis_index("fsdp")
    zh, x = island // 4, island % 4
    y, z, c = fsdp // 8, (fsdp // 2) % 4, fsdp % 2

    def at(zh_, x_, y_, z_, c_):
        return (zh_ * 4 + x_, y_ * 8 + z_ * 2 + c_)

    low = z < 2
    zm = jnp.where(low, z, 3 - z)

    def zo(j):
        if j == 0:
            return z
        m = j if j > 1 else jnp.where(zm == 0, 1, 0)
        return jnp.where(low, m, 3 - m)

    oz = [zo(j) for j in range(4)]
    y_up, y_dn, y_far = (y + 1) % 4, (y + 3) % 4, (y + 2) % 4
    has_up, has_dn = z < 3, z > 0
    z_up, z_dn = jnp.minimum(z + 1, 3), jnp.maximum(z - 1, 0)
    dev_yu, dev_yd, dev_yf = (at(zh, x, o, z, c) for o in (y_up, y_dn, y_far))
    dev_zu, dev_zd = at(zh, x, y, z_up, c), at(zh, x, y, z_dn, c)
    dev_z = [None] + [at(zh, x, y, oz[j], c) for j in (1, 2, 3)]
    dev_sib = at(zh, x, y, z, 1 - c)
    dev_far = at(1 - zh, x, y, z, c)
    dev_x = [at(zh, (x + d) % 4, y, z, c) for d in (1, 2, 3)]

    loads = [
        pltpu.make_async_copy(cur_hbm.at[0], cur4, load_sem.at[0]),
        pltpu.make_async_copy(anc_hbm, anc4, load_sem.at[1]),
        pltpu.make_async_copy(mom_hbm, mom4, load_sem.at[2]),
        pltpu.make_async_copy(tok_hbm, tok, load_sem.at[3]),
    ]
    for load in loads:
        load.start()

    barrier = pltpu.get_barrier_semaphore()
    peers = (*dev_x, dev_far, dev_yu, dev_yd, dev_yf, *dev_z[1:], dev_sib)
    for dev in peers:
        pl.semaphore_signal(barrier, inc=1, device_id=dev, device_id_type=MESH)

    fr = frag[0]
    loads[0].wait()
    whole = cur4[fr].reshape(16, G, WIDTH)
    cur[...] = whole
    ra[z, y] = whole[:HALF]
    pl.semaphore_wait(barrier, len(peers))

    def remote(src, dst, ss, rs, dev):
        return pltpu.make_async_remote_copy(
            src_ref=src, dst_ref=dst, send_sem=ss, recv_sem=rs,
            device_id=dev, device_id_type=MESH,
        )

    def raw_copy(k, d):
        to = (x + d + 1) % 4
        return remote(cur.at[4 * k + to], raw.at[d, k], raw_ss.at[d, k], raw_rs.at[d, k], dev_x[d])

    def send_raw(k):
        for d in range(3):
            raw_copy(k, d).start()

    def s_copy(k):
        return remote(s_out.at[k], s_in.at[k], s_ss.at[k], s_rs.at[k], dev_far)

    def d_copy(k, d):
        mine = 4 * k + x
        return remote(drift.at[mine], drift.at[mine], d_ss.at[d, k], d_rs.at[d, k], dev_x[d])

    def d_wait(k, d):
        theirs = 4 * k + (x + 3 - d) % 4
        remote(drift.at[theirs], drift.at[theirs], d_ss.at[d, k], d_rs.at[d, k], dev_x[d]).wait_recv()

    def island_sum(k):
        for d in range(3):
            raw_copy(k, d).wait_recv()
        mine = 4 * k + x
        anc = anc4[fr, pl.ds(pl.multiple_of(mine * G, G), G), :].astype(jnp.float32)
        total = cur[mine].astype(jnp.float32) - anc
        for d in range(3):
            total += raw[d, k].astype(jnp.float32) - anc
        s_out[k] = total.astype(jnp.bfloat16)
        s_copy(k).start()

    def step(anc, mom, mean):
        nxt = outer_momentum * mom + mean
        return nxt, anc + outer_rate * (outer_momentum * nxt + mean)

    def exchange(k):
        s_copy(k).wait_recv()
        both = s_out[k].astype(jnp.float32) + s_in[k].astype(jnp.float32)
        drift[4 * k + x] = both * 0.125

    def share(k):
        for d in range(3):
            d_copy(k, d).start()

    def own_global(k):
        rows = pl.ds(pl.multiple_of((4 * k + x) * G, G), G)
        _, glob = step(anc4[fr, rows, :].astype(jnp.float32), mom4[fr, rows, :], drift[4 * k + x])
        gb[z, x, y, k] = glob.astype(jnp.bfloat16)

    def own(k):
        for d in range(3):
            d_wait(k, d)
        rows = pl.ds(64 * k, 64)
        mean = drift[4 * k:4 * k + 4].reshape(64, WIDTH)
        nxt, glob = step(anc4[fr, rows, :].astype(jnp.float32), mom4[fr, rows, :], mean)
        local = cur[4 * k:4 * k + 4].reshape(64, WIDTH).astype(jnp.float32)
        new = (blend_local * local + (1.0 - blend_local) * glob).astype(jnp.bfloat16)
        if k >= 2:
            wb[z, c, y, 4 * k - 8:4 * k - 4] = new.reshape(4, G, WIDTH)
        return nxt, new

    def place(k, nxt, new):
        rows = pl.ds(64 * k, 64)
        for i in range(4):
            mom4[i, rows, :] = jnp.where(fr == i, nxt, mom4[i, rows, :])
            cur4[i, rows, :] = jnp.where(fr == i, new, cur4[i, rows, :])

    outs = [
        pltpu.make_async_copy(cur4, cur_out.at[0], out_sem.at[0]),
        pltpu.make_async_copy(mom4, mom_out, out_sem.at[1]),
    ]

    def block(kind, oy, ozj, span):
        if kind == 0:
            return ra.at[ozj, oy, pl.ds(*span)]
        return wb.at[ozj, c, oy, pl.ds(*span)]

    pieces, parts, arrived = (A_PIECES, B_PIECES), (A_PARTS, B_PARTS), (a_rs, b_rs)

    def go(t, dev, kind, oy, ozj, p, h, span):
        ref = block(kind, oy, ozj, span)
        return remote(ref, ref, send_sem.at[t], arrived[kind].at[ozj * 4 + oy, p, h], dev)

    def arrive(kind, oy, ozj, p, h, span):
        go(0, dev_yu, kind, oy, ozj, p, h, span).wait_recv()

    def to_y(kind, ozj, p):
        go(0, dev_yu, kind, y, ozj, p, 0, pieces[kind][p]).start()
        go(1, dev_yd, kind, y, ozj, p, 0, pieces[kind][p]).start()

    def to_z(kind, p, j):
        go(2, dev_z[j], kind, y, z, p, 0, pieces[kind][p]).start()

    def zz(kind, j, p):
        arrive(kind, y, oz[j], p, 0, pieces[kind][p])
        to_y(kind, oz[j], p)

    def zyd(kind, j, p):
        arrive(kind, y_dn, oz[j], p, 0, pieces[kind][p])
        go(0, dev_yu, kind, y_dn, oz[j], p, 0, parts[kind][p][0]).start()

    def zyu(kind, j, p):
        arrive(kind, y_up, oz[j], p, 0, pieces[kind][p])
        go(1, dev_yd, kind, y_up, oz[j], p, 1, parts[kind][p][1]).start()

    def zy_far(kind, j, p):
        for h in range(2):
            arrive(kind, y_far, oz[j], p, h, parts[kind][p][h])

    def onward(oy, ozj, up, dn):
        @pl.when(up)
        def _():
            go(3, dev_zu, 0, oy, ozj, YP, 0, A_PIECES[YP]).start()

        @pl.when(dn)
        def _():
            go(4, dev_zd, 0, oy, ozj, YP, 0, A_PIECES[YP]).start()

    def yz(j, oy):
        arrive(0, oy, oz[j], YP, 0, A_PIECES[YP])
        onward(oy, oz[j], (oz[j] < z) & has_up, (oz[j] > z) & has_dn)

    def g_copy(oy, ozj, dev):
        ref = gb.at[ozj, x, oy]
        return remote(ref, ref, send_sem.at[5], g_rs.at[ozj * 4 + oy], dev)

    def g_to_y(ozj):
        for dev in (dev_yu, dev_yd, dev_yf):
            g_copy(y, ozj, dev).start()

    def g_to_z():
        for dev in dev_z[1:]:
            g_copy(y, z, dev).start()

    def zzg(j):
        g_copy(y, oz[j], dev_yu).wait_recv()
        g_to_y(oz[j])

    def x_copy(j, d):
        ref = gb.at[oz[j], x]
        return remote(ref, ref, send_sem.at[6], x_rs.at[oz[j], d], dev_x[d])

    def xg(j):
        for oy in (y_up, y_dn, y_far):
            g_copy(oy, oz[j], dev_yu).wait_recv()
        for d in range(3):
            x_copy(j, d).start()

    def x_wait(j, d):
        ref = gb.at[oz[j], (x + 3 - d) % 4]
        remote(ref, ref, send_sem.at[6], x_rs.at[oz[j], d], dev_x[d]).wait_recv()

    def sib(kind, j):
        ref = (wa, wb)[kind].at[oz[j], c]
        return remote(ref, ref, send_sem.at[7], sib_rs.at[kind, oz[j]], dev_sib)

    def sib_wait(kind, j):
        ref = (wa, wb)[kind].at[oz[j], 1 - c]
        remote(ref, ref, send_sem.at[7], sib_rs.at[kind, oz[j]], dev_sib).wait_recv()

    def blend(j):
        zy_far(0, j, ZP)
        for d in range(3):
            x_wait(j, d)

        def one(oy, _):
            for k in range(2):
                for q in range(4):
                    mix = blend_local * ra[oz[j], oy, 4 * k + q].astype(jnp.float32)
                    mix += (1.0 - blend_local) * gb[oz[j], q, oy, k].astype(jnp.float32)
                    wa[oz[j], c, oy, 4 * k + q] = mix.astype(jnp.bfloat16)
            return 0

        lax.fori_loop(0, 4, one, 0)
        sib(0, j).start()

    def finish(j):
        for p in range(2):
            zy_far(1, j, p)
        sib(1, j).start()

    def multiply(kind, j):
        sib_wait(kind, j)

        cols = [
            pl.ds(pl.multiple_of((oy * 8 + oz[j] * 2 + core) * ROWS + kind * 128, 128), 128)
            for core in range(2) for oy in range(4)
        ]
        rhs = (wa, wb)[kind].at[oz[j]]
        a = jnp.concatenate([tok[:, col] for col in cols], axis=1)
        acc[...] += jnp.dot(a, rhs[...].reshape(1024, WIDTH), preferred_element_type=jnp.float32)

    acc[...] = jnp.zeros_like(acc)
    to_z(0, ZP, 1)
    to_z(0, ZP, 3)
    send_raw(1)
    to_y(0, z, 1)
    to_z(0, ZP, 2)
    send_raw(0)
    send_raw(2)
    loads[1].wait()
    island_sum(2)
    to_y(0, z, 0)
    send_raw(3)
    zyd(0, 0, 1)
    zyu(0, 0, 1)
    island_sum(0)
    island_sum(1)
    zz(0, 2, 0)
    zz(0, 1, 0)
    island_sum(3)
    exchange(2)
    zyd(0, 0, 0)
    exchange(1)
    share(2)
    exchange(0)
    loads[2].wait()
    own_global(1)
    own_global(0)
    g_to_z()
    g_to_y(z)
    zz(0, 3, 0)
    zy_far(0, 0, YP)
    exchange(3)
    onward(y_far, z, has_up, has_dn)
    share(3)
    onward(y, z, has_up, has_dn)
    zyu(0, 2, 0)
    share(1)
    zzg(1)
    own2 = own(2)
    onward(y_dn, z, has_up, has_dn)
    zzg(2)
    to_y(1, z, 0)
    onward(y_up, z, has_up, has_dn)
    to_z(1, 0, 2)
    own3 = own(3)
    to_z(1, 1, 1)
    share(0)
    own1 = own(1)
    zzg(3)
    yz(1, y)
    zyd(0, 1, 0)
    to_z(1, 0, 3)
    zyu(0, 0, 0)
    xg(0)
    zyd(1, 0, 0)
    zyu(0, 1, 0)
    to_y(1, z, 1)
    zz(1, 1, 1)
    xg(1)
    to_z(1, 0, 1)
    to_z(1, 1, 2)
    to_z(1, 1, 3)
    zz(1, 3, 0)
    place(1, *own1)
    xg(2)
    zz(1, 2, 0)
    yz(1, y_up)
    zyd(1, 0, 1)
    zz(1, 1, 0)
    xg(3)
    own0 = own(0)
    place(0, *own0)
    zyu(0, 3, 0)
    zyu(1, 1, 1)
    zz(1, 3, 1)
    yz(2, y_up)
    blend(0)
    zz(1, 2, 1)
    zyd(0, 2, 0)
    zyu(1, 0, 0)
    zyu(1, 3, 0)
    yz(1, y_far)
    zyd(1, 3, 0)
    place(2, *own2)
    yz(2, y_dn)
    yz(1, y_dn)
    zyd(1, 1, 1)
    zyd(1, 1, 0)
    yz(3, y)
    blend(1)
    yz(3, y_up)
    zyu(1, 0, 1)
    zyu(1, 2, 0)
    zyu(1, 1, 0)
    yz(3, y_far)
    zyd(1, 2, 0)
    zyu(1, 2, 1)
    zyd(1, 2, 1)
    zyd(1, 3, 1)
    zyu(1, 3, 1)
    place(3, *own3)
    zyd(0, 3, 0)
    yz(2, y_far)
    loads[3].wait()
    multiply(0, 0)
    yz(3, y_dn)
    multiply(0, 1)
    yz(2, y)
    finish(1)
    finish(2)
    finish(0)
    finish(3)
    blend(2)
    blend(3)
    multiply(1, 0)
    multiply(0, 2)
    multiply(0, 3)
    multiply(1, 1)
    multiply(1, 2)
    for out in outs:
        out.start()
    multiply(1, 3)
    keys_v[...] = (acc[...] * (1.0 / math.sqrt(D))).astype(jnp.bfloat16)
    last = pltpu.make_async_copy(keys_v, keys, out_sem.at[2])
    last.start()

    for k in range(CHUNKS):
        s_copy(k).wait_send()
        for d in range(3):
            raw_copy(k, d).wait_send()
            d_copy(k, d).wait_send()

    flat = wb.reshape(32 * HALF * G, WIDTH)

    def sent(t, groups):
        ref = flat.at[pl.ds(0, groups * G)]
        remote(ref, ref, send_sem.at[t], g_rs.at[0], dev_sib).wait_send()

    def size(kind, p, h=None):
        return pieces[kind][p][1] if h is None else parts[kind][p][h][1]

    zfirst = ((0, ZP), (1, 0), (1, 1))
    for h in range(2):
        sent(h, 4 * sum(size(*kp) + size(*kp, h) for kp in zfirst) + size(0, YP) + size(0, YP, h))
    sent(2, 3 * sum(size(*kp) for kp in zfirst))
    for at_z in range(3):
        @pl.when(z == at_z)
        def _(at_z=at_z):
            sent(3, (at_z + 1) * 4 * size(0, YP))

        @pl.when(z == 3 - at_z)
        def _(at_z=at_z):
            sent(4, (at_z + 1) * 4 * size(0, YP))
    sent(5, 2 * (3 + 3 * 4))
    sent(6, 4 * 3 * 8)
    sent(7, 2 * 4 * 4 * HALF)
    for out in outs:
        out.wait()
    last.wait()


def fused(current, anchor, momentum, tokens, fragment):
    bf, f32 = jnp.bfloat16, jnp.float32
    dma = pltpu.SemaphoreType.DMA
    return pl.pallas_call(
        kernel,
        out_shape=(
            jax.ShapeDtypeStruct((512, WIDTH), bf),
            jax.ShapeDtypeStruct((1, 4, ROWS, WIDTH), bf),
            jax.ShapeDtypeStruct((4, ROWS, WIDTH), f32),
        ),
        in_specs=[pl.BlockSpec(memory_space=pltpu.SMEM)] + [pl.BlockSpec(memory_space=pltpu.HBM)] * 4,
        out_specs=tuple([pl.BlockSpec(memory_space=pl.ANY)] * 3),
        scratch_shapes=[
            pltpu.VMEM((4, ROWS, WIDTH), bf),
            pltpu.VMEM((4, ROWS, WIDTH), bf),
            pltpu.VMEM((4, ROWS, WIDTH), f32),
            pltpu.VMEM((512, D), bf),
            pltpu.VMEM((4, 4, HALF, G, WIDTH), bf),
            pltpu.VMEM((4, 2, 4, HALF, G, WIDTH), bf),
            pltpu.VMEM((4, 2, 4, HALF, G, WIDTH), bf),
            pltpu.VMEM((4, 4, 4, 2, G, WIDTH), bf),
            pltpu.VMEM((16, G, WIDTH), bf),
            pltpu.VMEM((3, CHUNKS, G, WIDTH), bf),
            pltpu.VMEM((CHUNKS, G, WIDTH), bf),
            pltpu.VMEM((CHUNKS, G, WIDTH), bf),
            pltpu.VMEM((16, G, WIDTH), f32),
            pltpu.VMEM((512, WIDTH), bf),
            pltpu.VMEM((512, WIDTH), f32),
            dma((4,)), dma((3,)),
            dma((3, CHUNKS)), dma((3, CHUNKS)), dma((CHUNKS,)), dma((CHUNKS,)),
            dma((3, CHUNKS)), dma((3, CHUNKS)),
            dma((8,)), dma((16, 2, 2)), dma((16, 2, 2)), dma((16,)), dma((4, 3)), dma((2, 4)),
        ],
        compiler_params=pltpu.CompilerParams(
            collective_id=0, has_side_effects=True, vmem_limit_bytes=VMEM
        ),
    )(fragment, current, anchor, momentum, tokens)


def place_kernel(cur_in, mom_in, keys_in, cur, mom, keys):
    cur[...] = cur_in[...]
    mom[...] = mom_in[...]
    keys[...] = keys_in[...]


def local(current, anchor, momentum, tokens, fragment):
    keys, new_current, new_momentum = fused(current, anchor, momentum, tokens, fragment)
    shapes = [jax.ShapeDtypeStruct(a.shape, a.dtype) for a in (new_current, new_momentum, keys)]
    specs = [
        pl.BlockSpec((1, 4, ROWS // 2, WIDTH), lambda i: (0, 0, i, 0)),
        pl.BlockSpec((4, ROWS // 2, WIDTH), lambda i: (0, i, 0)),
        pl.BlockSpec((ROWS, WIDTH), lambda i: (i, 0)),
    ]
    return pl.pallas_call(
        place_kernel,
        out_shape=tuple(shapes),
        grid=(2,),
        in_specs=specs,
        out_specs=tuple(specs),
        compiler_params=pltpu.CompilerParams(vmem_limit_bytes=VMEM),
    )(new_current, new_momentum, keys)


def solution(mesh):
    placed = (
        P("island", None, "fsdp", None),
        P(None, "fsdp", None),
        P(None, "fsdp", None),
        P(("island", "fsdp"), None),
        P(),
    )
    return jax.shard_map(
        local,
        mesh=mesh,
        in_specs=placed,
        out_specs=(
            P("island", None, "fsdp", None),
            P(None, "fsdp", None),
            P(("island", "fsdp"), None),
        ),
        check_vma=False,
    )
```

time: 213 us -> 69.7 us (0.33)
  waiting for transfers between devices: 175 us -> 0 us
  Pallas kernels: 0 us -> 68.3 us
  between operations: 14.7 us -> 1.29 us
  matrix products: 11.1 us -> 0 us
  local copies, waits for them, and re-layouts: 7.31 us -> 0 us
  other arithmetic: 4.03 us -> 0 us
    psum x1 -> x0, waiting for transfers between devices: 107 us -> none  [synchronize(): drift_mean = lax.psum(drift_local, 'island') / islands]
    pallas_call x0 -> x2, Pallas kernels: none -> 68.3 us  [the longest x1 64.9 us: fused(): pl.pallas_call(kernel, out_shape=(jax.ShapeDtypeStruct((512, WIDTH), bf),...]
    all_gather x1 -> x0, waiting for transfers between devices: 68 us -> none  [synchronize(): lax.all_gather(blended, 'fsdp', axis=0, tiled=True)]
    dot_general x1 -> x0, matrix products: 11.1 us -> none  [synchronize(): jnp.dot(tokens, lax.all_gather(blended, 'fsdp', axis=0, tiled=True), pref...]
    unnamed x7 -> x0, local copies, waits for them, and re-layouts: 4.88 us -> none
    dynamic_update_slice x2 -> x0, local copies, waits for them, and re-layouts: 2.44 us -> none  [the longest x1 1.46 us: local(): lax.dynamic_update_index_in_dim(momentum, mom_next, slot_index, 0)]
    add x1 -> x0, other arithmetic: 2.2 us -> none  [synchronize(): mom_next = outer_momentum * mom_layer + drift_mean]
  transfers between devices with their start and end apart: 2 -> 0, of which waited for: 2 -> 0; matrix products, arithmetic and copies ran while one was open for 1% -> 0% of each run, Pallas kernels for 0% -> 0%
where the time goes in v3:
time: 69.7 us; the launch traced here: 69.6 us
  Pallas kernels  68.3 us (98%)
  between operations  1.29 us (2%)
    pallas_call x1, Pallas kernels, fused(): pl.pallas_call(kernel, out_shape=(jax.ShapeDtypeStruct((512, WIDTH), bf),...  64.9 us
    pallas_call x1, Pallas kernels, local(): pl.pallas_call(place_kernel, out_shape=tuple(shapes), grid=(2,), in_specs...  3.39 us

profile of v3, /device:TPU:1, one launch (start us, length us, event | category | flops | bytes accessed | tf_op | source)
XLA Modules:
  0.0 69.6 jit_solution(10092029452385759942)
XLA Ops:
  1.3 64.9 %shard_map.76 = (bf16[512,512]{1,0:T(8,128)(2,1)}, bf16[1,4,256,512]{3,2,1,0:T(8,128)(2,1)}, f32[4,256,512]{2,1,0:T(8,128)}) custom-call(s32[1]{0:T(128)S(6)} %copy.8.frag, bf16[1,4,256,512]{3,2,1,0:T(8,128)(2,1)} %cur_hbm.1, bf16[4,256,512]{2,1,0:T(8,128)(2,1)} %anc_hbm.1, f32[4,256,512]{2,1,0:T(8,128)} %mom_hbm.1, bf16[512,8192]{1,0:T(8,128)(2,1)} %tok_hbm.1), custom_call_target="tpu_custom_call" | custom-call | tf_op jit(solution)/shard_map/pallas_call | solution.py:443
  66.2 3.4 %shard_map.77 = (bf16[1,4,256,512]{3,2,1,0:T(8,128)(2,1)}, f32[4,256,512]{2,1,0:T(8,128)}, bf16[512,512]{1,0:T(8,128)(2,1)}) custom-call(bf16[1,4,256,512]{3,2,1,0:T(8,128)(2,1)} %get-tuple-element.6.cur_in, f32[4,256,512]{2,1,0:T(8,128)} %get-tuple-element.7.mom_in, bf16[512,512]{1,0:T(8,128)(2,1)} %get-tuple-element.8.keys_in), custom_call_target="tpu_custom_call" | custom-call | tf_op jit(solution)/shard_map/pallas_call | solution.py:493

commit v4 on v3

--- a/solution.py
+++ b/solution.py
@@ -29,7 +29,7 @@
            keys, cur_out, mom_out,
            cur4, anc4, mom4, tok, ra, wa, wb, gb, cur, raw, s_out, s_in, drift, keys_v, acc,
            load_sem, out_sem, raw_ss, raw_rs, s_ss, s_rs, d_ss, d_rs,
-           send_sem, a_rs, b_rs, g_rs, x_rs, sib_rs):
+           send_sem, a_rs, b_rs, g_rs, gh_rs, x_rs, xh_rs, sib_rs, sibb_rs):
     island = lax.axis_index("island")
     fsdp = lax.axis_index("fsdp")
     zh, x = island // 4, island % 4
@@ -51,7 +51,7 @@
     y_up, y_dn, y_far = (y + 1) % 4, (y + 3) % 4, (y + 2) % 4
     has_up, has_dn = z < 3, z > 0
     z_up, z_dn = jnp.minimum(z + 1, 3), jnp.maximum(z - 1, 0)
-    dev_yu, dev_yd, dev_yf = (at(zh, x, o, z, c) for o in (y_up, y_dn, y_far))
+    dev_yu, dev_yd = at(zh, x, y_up, z, c), at(zh, x, y_dn, z, c)
     dev_zu, dev_zd = at(zh, x, y, z_up, c), at(zh, x, y, z_dn, c)
     dev_z = [None] + [at(zh, x, y, oz[j], c) for j in (1, 2, 3)]
     dev_sib = at(zh, x, y, z, 1 - c)
@@ -68,7 +68,7 @@
         load.start()
 
     barrier = pltpu.get_barrier_semaphore()
-    peers = (*dev_x, dev_far, dev_yu, dev_yd, dev_yf, *dev_z[1:], dev_sib)
+    peers = (*dev_x, dev_far, dev_yu, dev_yd, *dev_z[1:], dev_sib)
     for dev in peers:
         pl.semaphore_signal(barrier, inc=1, device_id=dev, device_id_type=MESH)
 
@@ -210,9 +210,13 @@
         ref = gb.at[ozj, x, oy]
         return remote(ref, ref, send_sem.at[5], g_rs.at[ozj * 4 + oy], dev)
 
+    def g_part(oy, ozj, k, dev):
+        ref = gb.at[ozj, x, oy, k]
+        return remote(ref, ref, send_sem.at[5], gh_rs.at[ozj, k], dev)
+
     def g_to_y(ozj):
-        for dev in (dev_yu, dev_yd, dev_yf):
-            g_copy(y, ozj, dev).start()
+        g_copy(y, ozj, dev_yu).start()
+        g_copy(y, ozj, dev_yd).start()
 
     def g_to_z():
         for dev in dev_z[1:]:
@@ -222,32 +226,54 @@
         g_copy(y, oz[j], dev_yu).wait_recv()
         g_to_y(oz[j])
 
-    def x_copy(j, d):
-        ref = gb.at[oz[j], x]
-        return remote(ref, ref, send_sem.at[6], x_rs.at[oz[j], d], dev_x[d])
+    def gf(j):
+        g_copy(y_dn, oz[j], dev_yu).wait_recv()
+        g_part(y_dn, oz[j], 0, dev_yu).start()
+        g_copy(y_up, oz[j], dev_yu).wait_recv()
+        g_part(y_up, oz[j], 1, dev_yd).start()
+
+    def x_copy(j, d, slot, dev):
+        ref = gb.at[oz[j], slot]
+        return remote(ref, ref, send_sem.at[6], x_rs.at[oz[j], d], dev)
+
+    def x_part(j, d, slot, dev):
+        ref = gb.at[oz[j], slot, pl.ds(2 * d, 2)]
+        return remote(ref, ref, send_sem.at[6], xh_rs.at[oz[j], d], dev)
+
+    x_up, x_dn, x_far = (x + 1) % 4, (x + 3) % 4, (x + 2) % 4
 
     def xg(j):
-        for oy in (y_up, y_dn, y_far):
-            g_copy(oy, oz[j], dev_yu).wait_recv()
-        for d in range(3):
-            x_copy(j, d).start()
-
-    def x_wait(j, d):
-        ref = gb.at[oz[j], (x + 3 - d) % 4]
-        remote(ref, ref, send_sem.at[6], x_rs.at[oz[j], d], dev_x[d]).wait_recv()
-
-    def sib(kind, j):
-        ref = (wa, wb)[kind].at[oz[j], c]
-        return remote(ref, ref, send_sem.at[7], sib_rs.at[kind, oz[j]], dev_sib)
+        for k in range(2):
+            g_part(y_far, oz[j], k, dev_yu).wait_recv()
+        x_copy(j, 0, x, dev_x[0]).start()
+        x_copy(j, 1, x, dev_x[2]).start()
+
+    def xf(j):
+        x_copy(j, 0, x_dn, dev_x[0]).wait_recv()
+        x_part(j, 0, x_dn, dev_x[0]).start()
+        x_copy(j, 1, x_up, dev_x[0]).wait_recv()
+        x_part(j, 1, x_up, dev_x[2]).start()
+
+    def sib_a(j):
+        ref = wa.at[oz[j], c]
+        return remote(ref, ref, send_sem.at[7], sib_rs.at[oz[j]], dev_sib)
+
+    def sib_b(j, oy, core):
+        ref = wb.at[oz[j], core, oy]
+        return remote(ref, ref, send_sem.at[7], sibb_rs.at[oz[j], oy], dev_sib)
 
     def sib_wait(kind, j):
-        ref = (wa, wb)[kind].at[oz[j], 1 - c]
-        remote(ref, ref, send_sem.at[7], sib_rs.at[kind, oz[j]], dev_sib).wait_recv()
+        if kind == 0:
+            ref = wa.at[oz[j], 1 - c]
+            remote(ref, ref, send_sem.at[7], sib_rs.at[oz[j]], dev_sib).wait_recv()
+        else:
+            for oy in range(4):
+                sib_b(j, oy, 1 - c).wait_recv()
 
     def blend(j):
         zy_far(0, j, ZP)
-        for d in range(3):
-            x_wait(j, d)
+        for d in range(2):
+            x_part(j, d, x_far, dev_x[0]).wait_recv()
 
         def one(oy, _):
             for k in range(2):
@@ -258,12 +284,14 @@
             return 0
 
         lax.fori_loop(0, 4, one, 0)
-        sib(0, j).start()
-
-    def finish(j):
-        for p in range(2):
-            zy_far(1, j, p)
-        sib(1, j).start()
+        sib_a(j).start()
+
+    def finish(j, r):
+        oy = (y, y_up, y_far, y_dn)[r]
+        if r == 2:
+            for p in range(2):
+                zy_far(1, j, p)
+        sib_b(j, oy, c).start()
 
     def multiply(kind, j):
         sib_wait(kind, j)
@@ -277,126 +305,146 @@
         acc[...] += jnp.dot(a, rhs[...].reshape(1024, WIDTH), preferred_element_type=jnp.float32)
 
     acc[...] = jnp.zeros_like(acc)
-    to_z(0, ZP, 1)
-    to_z(0, ZP, 3)
+    send_raw(0)
+    to_z(0, 0, 2)
+    to_z(0, 0, 1)
     send_raw(1)
+    send_raw(3)
     to_y(0, z, 1)
-    to_z(0, ZP, 2)
-    send_raw(0)
     send_raw(2)
+    to_y(0, z, 0)
     loads[1].wait()
-    island_sum(2)
-    to_y(0, z, 0)
-    send_raw(3)
-    zyd(0, 0, 1)
-    zyu(0, 0, 1)
     island_sum(0)
     island_sum(1)
-    zz(0, 2, 0)
+    island_sum(3)
     zz(0, 1, 0)
-    island_sum(3)
+    zyu(0, 0, 1)
+    zyu(0, 0, 0)
+    island_sum(2)
+    zyd(0, 0, 0)
+    exchange(0)
+    share(0)
+    loads[2].wait()
+    own_global(0)
+    exchange(1)
+    own_global(1)
+    g_to_z()
+    zyd(0, 0, 1)
+    exchange(3)
+    g_to_y(z)
+    share(3)
+    zyu(0, 1, 0)
+    to_z(0, 0, 3)
+    zyd(0, 1, 0)
+    zzg(2)
     exchange(2)
-    zyd(0, 0, 0)
-    exchange(1)
+    zzg(1)
     share(2)
-    exchange(0)
-    loads[2].wait()
-    own_global(1)
-    own_global(0)
-    g_to_z()
-    g_to_y(z)
-    zz(0, 3, 0)
-    zy_far(0, 0, YP)
-    exchange(3)
-    onward(y_far, z, has_up, has_dn)
-    share(3)
-    onward(y, z, has_up, has_dn)
-    zyu(0, 2, 0)
-    share(1)
-    zzg(1)
-    own2 = own(2)
-    onward(y_dn, z, has_up, has_dn)
-    zzg(2)
-    to_y(1, z, 0)
-    onward(y_up, z, has_up, has_dn)
-    to_z(1, 0, 2)
+    gf(0)
+    zzg(3)
     own3 = own(3)
     to_z(1, 1, 1)
-    share(0)
+    to_y(1, z, 1)
+    share(1)
+    gf(2)
+    to_z(1, 1, 2)
+    zz(0, 2, 0)
+    to_z(1, 1, 3)
+    xg(0)
+    own2 = own(2)
+    to_y(1, z, 0)
+    gf(3)
+    zz(1, 2, 1)
+    onward(y, z, has_up, has_dn)
+    zz(0, 3, 0)
+    xg(2)
+    zyd(1, 0, 1)
+    to_z(1, 0, 1)
+    gf(1)
+    zy_far(0, 0, YP)
+    onward(y_dn, z, has_up, has_dn)
+    to_z(1, 0, 2)
+    xf(0)
     own1 = own(1)
-    zzg(3)
+    xg(3)
+    zyu(1, 0, 1)
+    to_z(1, 0, 3)
+    own0 = own(0)
+    zyd(1, 0, 0)
+    onward(y_up, z, has_up, has_dn)
+    zyu(1, 0, 0)
+    zz(1, 3, 1)
+    zz(1, 1, 0)
+    place(1, *own1)
+    onward(y_far, z, has_up, has_dn)
+    blend(0)
+    zz(1, 2, 0)
+    xg(1)
+    finish(2, 0)
+    zyu(0, 2, 0)
+    place(0, *own0)
+    place(3, *own3)
+    finish(0, 2)
+    zyd(0, 2, 0)
+    zz(1, 1, 1)
+    yz(2, y)
+    finish(0, 0)
+    loads[3].wait()
+    multiply(0, 0)
+    xf(2)
+    zyu(1, 2, 1)
+    zz(1, 3, 0)
+    yz(2, y_dn)
+    xf(3)
+    finish(1, 0)
+    zyd(1, 2, 1)
+    yz(1, y_dn)
     yz(1, y)
-    zyd(0, 1, 0)
-    to_z(1, 0, 3)
-    zyu(0, 0, 0)
-    xg(0)
-    zyd(1, 0, 0)
-    zyu(0, 1, 0)
-    to_y(1, z, 1)
-    zz(1, 1, 1)
-    xg(1)
-    to_z(1, 0, 1)
-    to_z(1, 1, 2)
-    to_z(1, 1, 3)
-    zz(1, 3, 0)
-    place(1, *own1)
-    xg(2)
-    zz(1, 2, 0)
+    finish(0, 3)
+    zyu(1, 2, 0)
+    zyd(1, 2, 0)
+    finish(0, 1)
+    finish(2, 1)
+    zyu(1, 1, 0)
+    yz(2, y_up)
+    zyd(0, 3, 0)
+    zyu(1, 3, 1)
+    zyd(1, 3, 1)
+    zyu(0, 3, 0)
+    zyd(1, 1, 0)
+    yz(1, y_far)
+    finish(3, 0)
+    finish(2, 3)
+    place(2, *own2)
     yz(1, y_up)
-    zyd(1, 0, 1)
-    zz(1, 1, 0)
-    xg(3)
-    own0 = own(0)
-    place(0, *own0)
-    zyu(0, 3, 0)
+    yz(2, y_far)
+    for out in outs:
+        out.start()
+    xf(1)
+    blend(2)
+    yz(3, y_dn)
     zyu(1, 1, 1)
-    zz(1, 3, 1)
-    yz(2, y_up)
-    blend(0)
-    zz(1, 2, 1)
-    zyd(0, 2, 0)
-    zyu(1, 0, 0)
+    multiply(1, 0)
+    zyd(1, 3, 0)
+    yz(3, y)
+    zyd(1, 1, 1)
+    finish(3, 3)
     zyu(1, 3, 0)
-    yz(1, y_far)
-    zyd(1, 3, 0)
-    place(2, *own2)
-    yz(2, y_dn)
-    yz(1, y_dn)
-    zyd(1, 1, 1)
-    zyd(1, 1, 0)
-    yz(3, y)
+    multiply(0, 2)
+    yz(3, y_far)
+    finish(1, 1)
+    finish(1, 3)
+    finish(2, 2)
+    finish(3, 1)
     blend(1)
     yz(3, y_up)
-    zyu(1, 0, 1)
-    zyu(1, 2, 0)
-    zyu(1, 1, 0)
-    yz(3, y_far)
-    zyd(1, 2, 0)
-    zyu(1, 2, 1)
-    zyd(1, 2, 1)
-    zyd(1, 3, 1)
-    zyu(1, 3, 1)
-    place(3, *own3)
-    zyd(0, 3, 0)
-    yz(2, y_far)
-    loads[3].wait()
-    multiply(0, 0)
-    yz(3, y_dn)
+    blend(3)
+    multiply(1, 2)
+    finish(3, 2)
+    finish(1, 2)
     multiply(0, 1)
-    yz(2, y)
-    finish(1)
-    finish(2)
-    finish(0)
-    finish(3)
-    blend(2)
-    blend(3)
-    multiply(1, 0)
-    multiply(0, 2)
     multiply(0, 3)
     multiply(1, 1)
-    multiply(1, 2)
-    for out in outs:
-        out.start()
     multiply(1, 3)
     keys_v[...] = (acc[...] * (1.0 / math.sqrt(D))).astype(jnp.bfloat16)
     last = pltpu.make_async_copy(keys_v, keys, out_sem.at[2])
@@ -429,8 +477,8 @@
         @pl.when(z == 3 - at_z)
         def _(at_z=at_z):
             sent(4, (at_z + 1) * 4 * size(0, YP))
-    sent(5, 2 * (3 + 3 * 4))
-    sent(6, 4 * 3 * 8)
+    sent(5, 3 * 2 + 4 * (2 * 2 + 2))
+    sent(6, 4 * (2 * 8 + 2 * 4))
     sent(7, 2 * 4 * 4 * HALF)
     for out in outs:
         out.wait()
@@ -468,7 +516,8 @@
             dma((4,)), dma((3,)),
             dma((3, CHUNKS)), dma((3, CHUNKS)), dma((CHUNKS,)), dma((CHUNKS,)),
             dma((3, CHUNKS)), dma((3, CHUNKS)),
-            dma((8,)), dma((16, 2, 2)), dma((16, 2, 2)), dma((16,)), dma((4, 3)), dma((2, 4)),
+            dma((8,)), dma((16, 2, 2)), dma((16, 2, 2)), dma((16,)), dma((4, 2)),
+            dma((4, 2)), dma((4, 2)), dma((4,)), dma((4, 4)),
         ],
         compiler_params=pltpu.CompilerParams(
             collective_id=0, has_side_effects=True, vmem_limit_bytes=VMEM

time: 69.7 us -> 64.9 us (0.931)
  Pallas kernels: 68.3 us -> 63.6 us
    pallas_call x1, Pallas kernels: 64.9 us -> 60.2 us  [fused(): pl.pallas_call(kernel, out_shape=(jax.ShapeDtypeStruct((512, WIDTH), bf),...]
where the time goes in v4:
time: 64.9 us; the launch traced here: 64.8 us
  Pallas kernels  63.6 us (98%)
  between operations  1.29 us (2%)
    pallas_call x1, Pallas kernels, fused(): pl.pallas_call(kernel, out_shape=(jax.ShapeDtypeStruct((512, WIDTH), bf),...  60.2 us
    pallas_call x1, Pallas kernels, local(): pl.pallas_call(place_kernel, out_shape=tuple(shapes), grid=(2,), in_specs...  3.39 us

profile of v4, /device:TPU:1, one launch (start us, length us, event | category | flops | bytes accessed | tf_op | source)
XLA Modules:
  0.0 64.8 jit_solution(6618682216110538148)
XLA Ops:
  1.3 60.2 %shard_map.76 = (bf16[512,512]{1,0:T(8,128)(2,1)}, bf16[1,4,256,512]{3,2,1,0:T(8,128)(2,1)}, f32[4,256,512]{2,1,0:T(8,128)}) custom-call(s32[1]{0:T(128)S(6)} %copy.8.frag, bf16[1,4,256,512]{3,2,1,0:T(8,128)(2,1)} %cur_hbm.1, bf16[4,256,512]{2,1,0:T(8,128)(2,1)} %anc_hbm.1, f32[4,256,512]{2,1,0:T(8,128)} %mom_hbm.1, bf16[512,8192]{1,0:T(8,128)(2,1)} %tok_hbm.1), custom_call_target="tpu_custom_call" | custom-call | tf_op jit(solution)/shard_map/pallas_call | solution.py:491
  61.5 3.4 %shard_map.77 = (bf16[1,4,256,512]{3,2,1,0:T(8,128)(2,1)}, f32[4,256,512]{2,1,0:T(8,128)}, bf16[512,512]{1,0:T(8,128)(2,1)}) custom-call(bf16[1,4,256,512]{3,2,1,0:T(8,128)(2,1)} %get-tuple-element.6.cur_in, f32[4,256,512]{2,1,0:T(8,128)} %get-tuple-element.7.mom_in, bf16[512,512]{1,0:T(8,128)(2,1)} %get-tuple-element.8.keys_in), custom_call_target="tpu_custom_call" | custom-call | tf_op jit(solution)/shard_map/pallas_call | solution.py:542

commit v5 on v4

--- a/solution.py
+++ b/solution.py
@@ -13,16 +13,16 @@
 G = 16
 CHUNKS = 4
 MESH = pl.DeviceIdType.MESH
-VMEM = 60 * 2**20
+VMEM = 54 * 2**20
 
 outer_momentum = 0.9
 outer_rate = 0.7
 blend_local = 0.5
 
 HALF = 8
-A_PIECES, A_PARTS = ((0, 5), (5, 3)), (((0, 3), (3, 2)), ((5, 1), (6, 2)))
+A_PIECES, A_PARTS = ((0, 2), (2, 3), (5, 3)), (((0, 1), (1, 1)), ((2, 2), (4, 1)), ((5, 1), (6, 2)))
 B_PIECES, B_PARTS = ((0, 4), (4, 4)), (((0, 2), (2, 2)), ((4, 2), (6, 2)))
-ZP, YP = 0, 1
+YP = 2
 
 
 def kernel(frag, cur_hbm, anc_hbm, mom_hbm, tok_hbm,
@@ -271,7 +271,8 @@
                 sib_b(j, oy, 1 - c).wait_recv()
 
     def blend(j):
-        zy_far(0, j, ZP)
+        for p in range(YP):
+            zy_far(0, j, p)
         for d in range(2):
             x_part(j, d, x_far, dev_x[0]).wait_recv()
 
@@ -306,146 +307,161 @@
 
     acc[...] = jnp.zeros_like(acc)
     send_raw(0)
-    to_z(0, 0, 2)
-    to_z(0, 0, 1)
+    to_y(0, z, 2)
+    to_z(0, 1, 1)
+    to_z(0, 1, 3)
     send_raw(1)
-    send_raw(3)
     to_y(0, z, 1)
     send_raw(2)
+    to_z(0, 0, 1)
+    to_z(0, 1, 2)
+    send_raw(3)
     to_y(0, z, 0)
     loads[1].wait()
     island_sum(0)
+    zz(0, 1, 1)
     island_sum(1)
+    zyd(0, 0, 2)
+    island_sum(2)
+    zz(0, 2, 1)
     island_sum(3)
+    zyu(0, 0, 2)
     zz(0, 1, 0)
-    zyu(0, 0, 1)
+    zyd(0, 0, 0)
+    zz(0, 3, 1)
+    zyd(0, 1, 1)
+    zyd(0, 0, 1)
+    to_z(0, 0, 2)
+    exchange(0)
     zyu(0, 0, 0)
-    island_sum(2)
-    zyd(0, 0, 0)
-    exchange(0)
-    share(0)
     loads[2].wait()
     own_global(0)
     exchange(1)
     own_global(1)
     g_to_z()
-    zyd(0, 0, 1)
+    onward(y, z, has_up, has_dn)
+    zy_far(0, 0, YP)
+    exchange(2)
+    g_to_y(z)
+    zyd(0, 1, 0)
+    to_z(0, 0, 3)
+    zyd(0, 2, 1)
+    share(2)
     exchange(3)
-    g_to_y(z)
+    zyu(0, 0, 1)
+    zyu(0, 2, 1)
+    zyu(0, 1, 1)
     share(3)
+    share(1)
+    zyd(0, 3, 1)
     zyu(0, 1, 0)
-    to_z(0, 0, 3)
-    zyd(0, 1, 0)
+    onward(y_up, z, has_up, has_dn)
+    share(0)
     zzg(2)
-    exchange(2)
+    gf(0)
     zzg(1)
-    share(2)
-    gf(0)
     zzg(3)
-    own3 = own(3)
-    to_z(1, 1, 1)
-    to_y(1, z, 1)
-    share(1)
-    gf(2)
-    to_z(1, 1, 2)
-    zz(0, 2, 0)
-    to_z(1, 1, 3)
-    xg(0)
     own2 = own(2)
     to_y(1, z, 0)
+    to_z(1, 0, 2)
+    gf(2)
+    zyu(0, 3, 1)
+    xg(0)
+    to_z(1, 0, 1)
+    own3 = own(3)
+    to_z(1, 0, 3)
+    place(3, *own3)
+    to_y(1, z, 1)
+    zz(0, 2, 0)
+    zz(0, 3, 0)
+    gf(1)
+    own1 = own(1)
+    to_z(1, 1, 1)
+    to_z(1, 1, 2)
+    finish(0, 0)
+    onward(y_far, z, has_up, has_dn)
+    zyu(1, 0, 0)
+    xg(2)
+    yz(1, y)
+    zyd(1, 0, 0)
     gf(3)
-    zz(1, 2, 1)
-    onward(y, z, has_up, has_dn)
-    zz(0, 3, 0)
-    xg(2)
     zyd(1, 0, 1)
-    to_z(1, 0, 1)
-    gf(1)
-    zy_far(0, 0, YP)
+    zyu(1, 0, 1)
+    zz(1, 2, 0)
+    xf(0)
+    own0 = own(0)
+    to_z(1, 1, 3)
+    zyd(0, 2, 0)
+    xg(1)
+    zz(1, 3, 0)
+    zz(1, 1, 0)
+    finish(0, 3)
     onward(y_dn, z, has_up, has_dn)
-    to_z(1, 0, 2)
-    xf(0)
-    own1 = own(1)
+    yz(2, y_up)
+    zz(1, 1, 1)
+    finish(0, 1)
     xg(3)
-    zyu(1, 0, 1)
-    to_z(1, 0, 3)
-    own0 = own(0)
-    zyd(1, 0, 0)
-    onward(y_up, z, has_up, has_dn)
-    zyu(1, 0, 0)
+    yz(2, y)
+    zyu(0, 2, 0)
+    blend(0)
+    finish(0, 2)
+    yz(1, y_far)
+    zyu(1, 2, 0)
     zz(1, 3, 1)
-    zz(1, 1, 0)
-    place(1, *own1)
-    onward(y_far, z, has_up, has_dn)
-    blend(0)
-    zz(1, 2, 0)
-    xg(1)
-    finish(2, 0)
-    zyu(0, 2, 0)
-    place(0, *own0)
-    place(3, *own3)
-    finish(0, 2)
-    zyd(0, 2, 0)
-    zz(1, 1, 1)
-    yz(2, y)
-    finish(0, 0)
+    finish(1, 0)
     loads[3].wait()
     multiply(0, 0)
+    xf(1)
+    zz(1, 2, 1)
+    zyd(1, 1, 0)
+    finish(3, 0)
+    zyd(0, 3, 0)
+    zyu(1, 1, 0)
+    place(0, *own0)
     xf(2)
-    zyu(1, 2, 1)
-    zz(1, 3, 0)
-    yz(2, y_dn)
+    yz(2, y_far)
+    multiply(1, 0)
+    place(1, *own1)
+    zyu(1, 1, 1)
+    zyd(1, 3, 0)
+    yz(3, y)
+    zyu(0, 3, 0)
+    finish(1, 1)
+    yz(1, y_dn)
+    zyd(1, 1, 1)
     xf(3)
-    finish(1, 0)
-    zyd(1, 2, 1)
-    yz(1, y_dn)
-    yz(1, y)
-    finish(0, 3)
-    zyu(1, 2, 0)
-    zyd(1, 2, 0)
-    finish(0, 1)
-    finish(2, 1)
-    zyu(1, 1, 0)
-    yz(2, y_up)
-    zyd(0, 3, 0)
-    zyu(1, 3, 1)
+    zyu(1, 3, 0)
+    place(2, *own2)
     zyd(1, 3, 1)
-    zyu(0, 3, 0)
-    zyd(1, 1, 0)
-    yz(1, y_far)
-    finish(3, 0)
-    finish(2, 3)
-    place(2, *own2)
     yz(1, y_up)
-    yz(2, y_far)
     for out in outs:
         out.start()
-    xf(1)
+    zyd(1, 2, 0)
+    finish(2, 0)
+    yz(2, y_dn)
+    blend(1)
+    zyu(1, 3, 1)
+    finish(1, 3)
+    zyd(1, 2, 1)
+    yz(3, y_far)
+    finish(3, 3)
+    finish(2, 3)
+    finish(3, 1)
+    zyu(1, 2, 1)
     blend(2)
     yz(3, y_dn)
-    zyu(1, 1, 1)
-    multiply(1, 0)
-    zyd(1, 3, 0)
-    yz(3, y)
-    zyd(1, 1, 1)
-    finish(3, 3)
-    zyu(1, 3, 0)
-    multiply(0, 2)
-    yz(3, y_far)
-    finish(1, 1)
-    finish(1, 3)
-    finish(2, 2)
-    finish(3, 1)
-    blend(1)
+    finish(2, 1)
+    multiply(0, 1)
+    finish(1, 2)
     yz(3, y_up)
     blend(3)
-    multiply(1, 2)
     finish(3, 2)
-    finish(1, 2)
-    multiply(0, 1)
-    multiply(0, 3)
+    multiply(0, 2)
+    finish(2, 2)
     multiply(1, 1)
     multiply(1, 3)
+    multiply(0, 3)
+    multiply(1, 2)
     keys_v[...] = (acc[...] * (1.0 / math.sqrt(D))).astype(jnp.bfloat16)
     last = pltpu.make_async_copy(keys_v, keys, out_sem.at[2])
     last.start()
@@ -465,7 +481,7 @@
     def size(kind, p, h=None):
         return pieces[kind][p][1] if h is None else parts[kind][p][h][1]
 
-    zfirst = ((0, ZP), (1, 0), (1, 1))
+    zfirst = ((0, 0), (0, 1), (1, 0), (1, 1))
     for h in range(2):
         sent(h, 4 * sum(size(*kp) + size(*kp, h) for kp in zfirst) + size(0, YP) + size(0, YP, h))
     sent(2, 3 * sum(size(*kp) for kp in zfirst))
@@ -491,9 +507,9 @@
     return pl.pallas_call(
         kernel,
         out_shape=(
-            jax.ShapeDtypeStruct((512, WIDTH), bf),
-            jax.ShapeDtypeStruct((1, 4, ROWS, WIDTH), bf),
-            jax.ShapeDtypeStruct((4, ROWS, WIDTH), f32),
+            pltpu.VMEM((512, WIDTH), bf),
+            pltpu.VMEM((1, 4, ROWS, WIDTH), bf),
+            pltpu.VMEM((4, ROWS, WIDTH), f32),
         ),
         in_specs=[pl.BlockSpec(memory_space=pltpu.SMEM)] + [pl.BlockSpec(memory_space=pltpu.HBM)] * 4,
         out_specs=tuple([pl.BlockSpec(memory_space=pl.ANY)] * 3),
@@ -516,7 +532,7 @@
             dma((4,)), dma((3,)),
             dma((3, CHUNKS)), dma((3, CHUNKS)), dma((CHUNKS,)), dma((CHUNKS,)),
             dma((3, CHUNKS)), dma((3, CHUNKS)),
-            dma((8,)), dma((16, 2, 2)), dma((16, 2, 2)), dma((16,)), dma((4, 2)),
+            dma((8,)), dma((16, 3, 2)), dma((16, 2, 2)), dma((16,)), dma((4, 2)),
             dma((4, 2)), dma((4, 2)), dma((4,)), dma((4, 4)),
         ],
         compiler_params=pltpu.CompilerParams(
@@ -525,27 +541,27 @@
     )(fragment, current, anchor, momentum, tokens)
 
 
-def place_kernel(cur_in, mom_in, keys_in, cur, mom, keys):
-    cur[...] = cur_in[...]
-    mom[...] = mom_in[...]
-    keys[...] = keys_in[...]
+def place_kernel(cur_in, mom_in, keys_in, cur, mom, keys, sem):
+    moves = [(mom_in.at[i], mom.at[i]) for i in range(4)]
+    moves += [(cur_in.at[0, pl.ds(2 * i, 2)], cur.at[0, pl.ds(2 * i, 2)]) for i in range(2)]
+    moves += [(keys_in, keys)]
+    copies = [pltpu.make_async_copy(a, b, sem.at[i]) for i, (a, b) in enumerate(moves)]
+    for copy in copies:
+        copy.start()
+    for copy in copies:
+        copy.wait()
 
 
 def local(current, anchor, momentum, tokens, fragment):
     keys, new_current, new_momentum = fused(current, anchor, momentum, tokens, fragment)
-    shapes = [jax.ShapeDtypeStruct(a.shape, a.dtype) for a in (new_current, new_momentum, keys)]
-    specs = [
-        pl.BlockSpec((1, 4, ROWS // 2, WIDTH), lambda i: (0, 0, i, 0)),
-        pl.BlockSpec((4, ROWS // 2, WIDTH), lambda i: (0, i, 0)),
-        pl.BlockSpec((ROWS, WIDTH), lambda i: (i, 0)),
-    ]
+    shapes = [jax.ShapeDtypeStruct(a.shape, a.dtype) for a in (current, momentum, keys)]
     return pl.pallas_call(
         place_kernel,
         out_shape=tuple(shapes),
-        grid=(2,),
-        in_specs=specs,
-        out_specs=tuple(specs),
-        compiler_params=pltpu.CompilerParams(vmem_limit_bytes=VMEM),
+        in_specs=[pl.BlockSpec(memory_space=pl.ANY)] * 3,
+        out_specs=tuple([pl.BlockSpec(memory_space=pl.ANY)] * 3),
+        scratch_shapes=[pltpu.SemaphoreType.DMA((7,))],
+        compiler_params=pltpu.CompilerParams(vmem_limit_bytes=16 * 2**20),
     )(new_current, new_momentum, keys)
 
 

time: 64.9 us -> 60.6 us (0.934)
  Pallas kernels: 63.6 us -> 59.2 us
    pallas_call x2, Pallas kernels: 63.6 us -> 59.2 us  [the longest x1 57.3 us: fused(): pl.pallas_call(kernel, out_shape=(pltpu.VMEM((512, WIDTH), bf), pltpu.VME...]
where the time goes in v5:
time: 60.6 us; the launch traced here: 60.5 us
  Pallas kernels  59.2 us (98%)
  between operations  1.29 us (2%)
    pallas_call x1, Pallas kernels, fused(): pl.pallas_call(kernel, out_shape=(pltpu.VMEM((512, WIDTH), bf), pltpu.VME...  57.3 us
    pallas_call x1, Pallas kernels, local(): pl.pallas_call(place_kernel, out_shape=tuple(shapes), in_specs=[pl.BlockS...  1.89 us

profile of v5, /device:TPU:1, one launch (start us, length us, event | category | flops | bytes accessed | tf_op | source)
XLA Modules:
  0.0 60.5 jit_solution(14499829185984940862)
XLA Ops:
  1.3 57.3 %shard_map.76 = (bf16[512,512]{1,0:T(8,128)(2,1)S(1)}, bf16[1,4,256,512]{3,2,1,0:T(8,128)(2,1)S(1)}, f32[4,256,512]{2,1,0:T(8,128)S(1)}) custom-call(s32[1]{0:T(128)S(6)} %copy.8.frag, bf16[1,4,256,512]{3,2,1,0:T(8,128)(2,1)} %cur_hbm.1, bf16[4,256,512]{2,1,0:T(8,128)(2,1)} %anc_hbm.1, f32[4,256,512]{2,1,0:T(8,128)} %mom_hbm.1, bf16[512,8192]{1,0:T(8,128)(2,1)} %tok_hbm.1), custom_call_target="tpu_custom_call" | custom-call | tf_op jit(solution)/shard_map/pallas_call | solution.py:507
  58.6 1.9 %shard_map.77 = (bf16[1,4,256,512]{3,2,1,0:T(8,128)(2,1)}, f32[4,256,512]{2,1,0:T(8,128)}, bf16[512,512]{1,0:T(8,128)(2,1)}) custom-call(bf16[1,4,256,512]{3,2,1,0:T(8,128)(2,1)S(1)} %get-tuple-element.6.cur_in, f32[4,256,512]{2,1,0:T(8,128)S(1)} %get-tuple-element.7.mom_in, bf16[512,512]{1,0:T(8,128)(2,1)S(1)} %get-tuple-element.8.keys_in), custom_call_target="tpu_custom_call" | custom-call | tf_op jit(solution)/shard_map/pallas_call | solution.py:558

commit v6 on v5

--- a/solution.py
+++ b/solution.py
@@ -27,7 +27,7 @@
 
 def kernel(frag, cur_hbm, anc_hbm, mom_hbm, tok_hbm,
            keys, cur_out, mom_out,
-           cur4, anc4, mom4, tok, ra, wa, wb, gb, cur, raw, s_out, s_in, drift, keys_v, acc,
+           cur4, anc4, mom4, tok, ra, wa, wb, gb, cur, raw, s_out, s_in, drift, acc,
            load_sem, out_sem, raw_ss, raw_rs, s_ss, s_rs, d_ss, d_rs,
            send_sem, a_rs, b_rs, g_rs, gh_rs, x_rs, xh_rs, sib_rs, sibb_rs):
     island = lax.axis_index("island")
@@ -294,7 +294,7 @@
                 zy_far(1, j, p)
         sib_b(j, oy, c).start()
 
-    def multiply(kind, j):
+    def multiply(kind, j, last=False):
         sib_wait(kind, j)
 
         cols = [
@@ -303,7 +303,23 @@
         ]
         rhs = (wa, wb)[kind].at[oz[j]]
         a = jnp.concatenate([tok[:, col] for col in cols], axis=1)
-        acc[...] += jnp.dot(a, rhs[...].reshape(1024, WIDTH), preferred_element_type=jnp.float32)
+        total = acc[...] + jnp.dot(a, rhs[...].reshape(1024, WIDTH), preferred_element_type=jnp.float32)
+        if last:
+            keys[...] = (total * (1.0 / math.sqrt(D))).astype(jnp.bfloat16)
+        else:
+            acc[...] = total
+
+    def left_early():
+        for k in range(CHUNKS):
+            s_copy(k).wait_send()
+            for d in range(3):
+                raw_copy(k, d).wait_send()
+
+    def left_shares():
+        for k in range(CHUNKS):
+            for d in range(3):
+                d_copy(k, d).wait_send()
+
 
     acc[...] = jnp.zeros_like(acc)
     send_raw(0)
@@ -458,19 +474,12 @@
     finish(3, 2)
     multiply(0, 2)
     finish(2, 2)
+    left_early()
     multiply(1, 1)
+    left_shares()
     multiply(1, 3)
     multiply(0, 3)
-    multiply(1, 2)
-    keys_v[...] = (acc[...] * (1.0 / math.sqrt(D))).astype(jnp.bfloat16)
-    last = pltpu.make_async_copy(keys_v, keys, out_sem.at[2])
-    last.start()
-
-    for k in range(CHUNKS):
-        s_copy(k).wait_send()
-        for d in range(3):
-            raw_copy(k, d).wait_send()
-            d_copy(k, d).wait_send()
+    multiply(1, 2, True)
 
     flat = wb.reshape(32 * HALF * G, WIDTH)
 
@@ -498,7 +507,6 @@
     sent(7, 2 * 4 * 4 * HALF)
     for out in outs:
         out.wait()
-    last.wait()
 
 
 def fused(current, anchor, momentum, tokens, fragment):
@@ -512,7 +520,7 @@
             pltpu.VMEM((4, ROWS, WIDTH), f32),
         ),
         in_specs=[pl.BlockSpec(memory_space=pltpu.SMEM)] + [pl.BlockSpec(memory_space=pltpu.HBM)] * 4,
-        out_specs=tuple([pl.BlockSpec(memory_space=pl.ANY)] * 3),
+        out_specs=(pl.BlockSpec(memory_space=pltpu.VMEM),) + tuple([pl.BlockSpec(memory_space=pl.ANY)] * 2),
         scratch_shapes=[
             pltpu.VMEM((4, ROWS, WIDTH), bf),
             pltpu.VMEM((4, ROWS, WIDTH), bf),
@@ -527,9 +535,8 @@
             pltpu.VMEM((CHUNKS, G, WIDTH), bf),
             pltpu.VMEM((CHUNKS, G, WIDTH), bf),
             pltpu.VMEM((16, G, WIDTH), f32),
-            pltpu.VMEM((512, WIDTH), bf),
             pltpu.VMEM((512, WIDTH), f32),
-            dma((4,)), dma((3,)),
+            dma((4,)), dma((2,)),
             dma((3, CHUNKS)), dma((3, CHUNKS)), dma((CHUNKS,)), dma((CHUNKS,)),
             dma((3, CHUNKS)), dma((3, CHUNKS)),
             dma((8,)), dma((16, 3, 2)), dma((16, 2, 2)), dma((16,)), dma((4, 2)),
@@ -542,9 +549,7 @@
 
 
 def place_kernel(cur_in, mom_in, keys_in, cur, mom, keys, sem):
-    moves = [(mom_in.at[i], mom.at[i]) for i in range(4)]
-    moves += [(cur_in.at[0, pl.ds(2 * i, 2)], cur.at[0, pl.ds(2 * i, 2)]) for i in range(2)]
-    moves += [(keys_in, keys)]
+    moves = ((mom_in, mom), (cur_in, cur), (keys_in, keys))
     copies = [pltpu.make_async_copy(a, b, sem.at[i]) for i, (a, b) in enumerate(moves)]
     for copy in copies:
         copy.start()
@@ -560,7 +565,7 @@
         out_shape=tuple(shapes),
         in_specs=[pl.BlockSpec(memory_space=pl.ANY)] * 3,
         out_specs=tuple([pl.BlockSpec(memory_space=pl.ANY)] * 3),
-        scratch_shapes=[pltpu.SemaphoreType.DMA((7,))],
+        scratch_shapes=[pltpu.SemaphoreType.DMA((3,))],
         compiler_params=pltpu.CompilerParams(vmem_limit_bytes=16 * 2**20),
     )(new_current, new_momentum, keys)
 

time: 60.6 us -> 60.4 us (level)
  no operation moved by 1% of the time
where the time goes in v6:
time: 60.4 us; the launch traced here: 60.3 us
  Pallas kernels  59 us (98%)
  between operations  1.29 us (2%)
    pallas_call x1, Pallas kernels, fused(): pl.pallas_call(kernel, out_shape=(pltpu.VMEM((512, WIDTH), bf), pltpu.VME...  57.2 us
    pallas_call x1, Pallas kernels, local(): pl.pallas_call(place_kernel, out_shape=tuple(shapes), in_specs=[pl.BlockS...  1.86 us

profile of v6, /device:TPU:1, one launch (start us, length us, event | category | flops | bytes accessed | tf_op | source)
XLA Modules:
  0.0 60.3 jit_solution(16727526809194029484)
XLA Ops:
  1.3 57.2 %shard_map.76 = (bf16[512,512]{1,0:T(8,128)(2,1)S(1)}, bf16[1,4,256,512]{3,2,1,0:T(8,128)(2,1)S(1)}, f32[4,256,512]{2,1,0:T(8,128)S(1)}) custom-call(s32[1]{0:T(128)S(6)} %copy.8.frag, bf16[1,4,256,512]{3,2,1,0:T(8,128)(2,1)} %cur_hbm.1, bf16[4,256,512]{2,1,0:T(8,128)(2,1)} %anc_hbm.1, f32[4,256,512]{2,1,0:T(8,128)} %mom_hbm.1, bf16[512,8192]{1,0:T(8,128)(2,1)} %tok_hbm.1), custom_call_target="tpu_custom_call" | custom-call | tf_op jit(solution)/shard_map/pallas_call | solution.py:515
  58.5 1.9 %shard_map.77 = (bf16[1,4,256,512]{3,2,1,0:T(8,128)(2,1)}, f32[4,256,512]{2,1,0:T(8,128)}, bf16[512,512]{1,0:T(8,128)(2,1)}) custom-call(bf16[1,4,256,512]{3,2,1,0:T(8,128)(2,1)S(1)} %get-tuple-element.6.cur_in, f32[4,256,512]{2,1,0:T(8,128)S(1)} %get-tuple-element.7.mom_in, bf16[512,512]{1,0:T(8,128)(2,1)S(1)} %get-tuple-element.8.keys_in), custom_call_target="tpu_custom_call" | custom-call | tf_op jit(solution)/shard_map/pallas_call | solution.py:563
